TPU v7x, 512 devices: a whole 4x4x16 slice. The times are simulated.
512 devices in a mesh: section: 16 (over z), peer: 32 (over y, x, core).
Axes of the slice: x: 4, y: 4, z: 16, core: 2. Of those that a mesh axis runs over, the one named last changes fastest.
Arguments:
- emitted: bfloat16 [16, 32, 128, 5120], P('section', 'peer'), may hold values from -6 to 6
- out_grads: bfloat16 [16, 32, 128, 5120], P('section', 'peer'), may hold values from -6 to 6
- adapter_in: bfloat16 [16, 16, 5120], P('section'), may hold values from -0.078125 to 0.078125
- adapter_out: bfloat16 [16, 16, 5120], P('section'), may hold values from -0.375 to 0.375
- wiring: int32 [16, 32, 32, 1], P('section', 'peer'), may hold values from 0 to 31; in each aligned block of 32 rows (0 to 31, 32 to 63, ..., all dimensions but the last counted through in order) no two rows name the same one
- counts: int32 [16, 32], P('section', 'peer'), may hold values from 24 to 32
Outputs:
- row_grads: bfloat16 [16, 32, 128, 5120], P('section', 'peer')
- grad_in: float32 [16, 16, 5120], P('section')
- grad_out: float32 [16, 16, 5120], P('section')
Inputs may be any that keep to these rules, and one draw needn't show every extreme that they name: `wiring`: on every peer of every section the 32 blocks name each peer exactly 1 times.
All inputs are finite; a program needn't handle non-finite values.
Results may differ from a plain program's by a relative error of at most 0.0053.
Values may be sent and summed in bfloat16 or wider, within the bound.
No kernel may reach another device: no remote copies, remote signals or barrier semaphores. Data moves between devices by JAX's collectives and lax.ppermute only.
A program may use at most 64 MiB of HBM per device.

v0:
```python
import jax
import jax.numpy as jnp
from jax import lax
from jax.sharding import PartitionSpec as P

EPS = 1e-06


def shifted(block, axis, distance):
    devices = range(lax.axis_size(axis))
    route = [(i - distance, i) for i in devices if i - distance in devices]
    return lax.ppermute(block, axis, route)


def adapter_backward(own_rows, out_rows, row_mask, weight_in, weight_out):
    rows_float = own_rows.astype(jnp.float32)
    inv_rms = lax.rsqrt(jnp.mean(rows_float * rows_float, axis=-1, keepdims=True) + EPS)
    normed_float = rows_float * inv_rms
    normed = normed_float.astype(jnp.bfloat16)
    preact = lax.dot_general(
        normed, weight_in, (((1,), (1,)), ((), ())), preferred_element_type=jnp.float32
    )
    activated = jax.nn.silu(preact).astype(jnp.bfloat16)
    masked = (out_rows.astype(jnp.float32) * row_mask).astype(jnp.bfloat16)
    grad_act = lax.dot_general(
        masked, weight_out, (((1,), (1,)), ((), ())), preferred_element_type=jnp.float32
    )
    gate_sig = jax.nn.sigmoid(preact)
    grad_pre = (grad_act * gate_sig * (1.0 + preact * (1.0 - gate_sig))).astype(jnp.bfloat16)
    grad_out = lax.dot_general(
        activated, masked, (((0,), (0,)), ((), ())), preferred_element_type=jnp.float32
    )
    grad_in = lax.dot_general(
        grad_pre, normed, (((0,), (0,)), ((), ())), preferred_element_type=jnp.float32
    )
    grad_norm = jnp.dot(grad_pre, weight_in, preferred_element_type=jnp.float32)
    centred = jnp.mean(grad_norm * normed_float, axis=-1, keepdims=True)
    row_grads = masked.astype(jnp.float32) + inv_rms * (grad_norm - normed_float * centred)
    return (row_grads.astype(jnp.bfloat16), grad_in, grad_out)


def shards(emitted, out_grads, adapter_in, adapter_out, wiring, counts):
    peer_count = lax.axis_size("peer")
    own_rows = emitted[0, 0]
    row_total = own_rows.shape[0]
    feature_width = own_rows.shape[1]
    blocks = wiring.shape[2]
    per_pair = blocks // peer_count
    block_rows = row_total // blocks
    targets = wiring[0, 0, :, 0]
    order = jnp.arange(blocks, dtype=jnp.int32)
    matches = targets[:, None] == targets[None, :]
    earlier = order[None, :] < order[:, None]
    slot_rank = jnp.sum(jnp.where(matches & earlier, 1, 0), axis=1).astype(jnp.int32)
    position = targets * per_pair + slot_rank
    placement = (position[:, None] == order[None, :]).astype(jnp.bfloat16)
    active = (order < counts[0, 0]).astype(jnp.float32)
    outgoing = jnp.dot(
        placement.T,
        own_rows.reshape(blocks, block_rows * feature_width),
        preferred_element_type=jnp.float32,
    ).astype(jnp.bfloat16)
    outgoing = outgoing.reshape(peer_count, per_pair * block_rows, feature_width)
    slot_live = jnp.dot(active, placement.astype(jnp.float32))
    live_rows = (
        jnp.repeat(slot_live, block_rows)
        .reshape(peer_count, per_pair * block_rows)
        .astype(jnp.bfloat16)
    )
    moved_rows, moved_live = shifted((outgoing, live_rows), "section", 1)
    routed_rows, routed_live = (
        lax.all_to_all(moved_rows, "peer", split_axis=0, concat_axis=0, tiled=True),
        lax.all_to_all(moved_live, "peer", split_axis=0, concat_axis=0, tiled=True),
    )
    received = routed_rows.reshape(row_total, feature_width)
    row_mask = routed_live.reshape(row_total, 1).astype(jnp.float32)
    grads_here, grad_in, grad_out = adapter_backward(
        received, out_grads[0, 0], row_mask, adapter_in[0], adapter_out[0]
    )
    grad_in, grad_out = lax.psum((grad_in, grad_out), "peer")
    returned = lax.all_to_all(
        grads_here.reshape(peer_count, per_pair * block_rows, feature_width),
        "peer",
        split_axis=0,
        concat_axis=0,
        tiled=True,
    )
    arrived = shifted(returned, "section", -1)
    row_grads = jnp.dot(
        placement,
        arrived.reshape(blocks, block_rows * feature_width),
        preferred_element_type=jnp.float32,
    ).astype(jnp.bfloat16)
    row_grads = row_grads.reshape(row_total, feature_width)
    return (
        row_grads.reshape(1, 1, row_total, feature_width),
        (grad_in / row_total).reshape(1, grad_in.shape[0], feature_width),
        (grad_out / row_total).reshape(1, grad_out.shape[0], feature_width),
    )


def solution(mesh):
    return jax.shard_map(
        shards,
        mesh=mesh,
        in_specs=(
            P("section", "peer", None, None),
            P("section", "peer", None, None),
            P("section", None, None),
            P("section", None, None),
            P("section", "peer", None, None),
            P("section", "peer"),
        ),
        out_specs=(
            P("section", "peer", None, None),
            P("section", None, None),
            P("section", None, None),
        ),
        check_vma=False,
    )
```

profile of v0, /device:TPU:1, one launch (start us, length us, event | category | flops | bytes accessed | tf_op | source)
XLA Modules:
  0.0 258.6 jit_solution(18055418441980678796)
XLA Ops:
  7.2 2.2 reshape_squeeze.3
  9.6 0.6 convolution_convert_fusion.1
  10.2 1.0 reshape.83
  11.2 5.4 %collective-permute-start.1 = (bf16[32,4,5120]{2,1,0:T(4,128)(2,1)S(1)}, bf16[32,4,5120]{2,1,0:T(4,128)(2,1)}, u32[]{:S(2)}, u32[]{:S(2)}) collective-permute-start(bf16[32,4,5120]{2,1,0:T(4,128)(2,1)S(1)} %reshape.83), channel_id=1, source_target_pairs={{0,32},{32,64},{64,96},{96,128},{128,160},{160,192},{192,224},{224... | collective-permute-start | bytes 3932168 | tf_op jit(solution)/shard_map/ppermute | solution.py:12
  17.5 2.5 collective-permute-start
  20.0 20.2 %collective-permute-done = bf16[32,4]{0,1:T(4,128)(2,1)S(1)} collective-permute-done((bf16[32,4]{0,1:T(4,128)(2,1)S(1)}, bf16[32,4]{0,1:T(4,128)(2,1)S(1)}, u32[]{:S(2)}, u32[]{:S(2)}) %collective-permute-start) | collective-permute-done | bytes 288 | tf_op jit(solution)/shard_map/ppermute | solution.py:12
  40.3 18.3 %all_to_all.19 = bf16[32,1,4]{2,1,0:T(2,128)(2,1)S(1)} all-to-all(bf16[32,1,4]{2,1,0:T(2,128)(2,1)S(1)} %copy.12), channel_id=1, replica_groups=mesh['section'=16,'peer'=32] {'peer'}, dimensions={0} | all-to-all | bytes 512 | tf_op jit(solution)/shard_map/all_to_all | solution.py:73
  58.6 4.3 %all-to-all-start.1 = ((bf16[32,4,5120]{2,1,0:T(4,128)(2,1)}), bf16[32,4,5120]{2,1,0:T(4,128)(2,1)S(1)}, u32[]{:S(2)}, u32[]{:S(2)}) async-start(bf16[32,4,5120]{2,1,0:T(4,128)(2,1)} %collective-permute-done.1), calls=%async_computation.1 | async-start | bytes 2621440 | tf_op jit(solution)/shard_map/all_to_all | solution.py:72
  63.0 19.0 %all-to-all-done.1 = bf16[32,4,5120]{2,1,0:T(4,128)(2,1)S(1)} async-done(((bf16[32,4,5120]{2,1,0:T(4,128)(2,1)}), bf16[32,4,5120]{2,1,0:T(4,128)(2,1)S(1)}, u32[]{:S(2)}, u32[]{:S(2)}) %all-to-all-start.1) | async-done | bytes 1310752 | tf_op jit(solution)/shard_map/all_to_all | solution.py:72
  82.0 0.8 multiply_reduce_fusion.1
  83.5 1.2 convert_element_type.84
  84.7 1.9 fusion.23
  87.1 2.4 reshape.90
  90.2 0.7 copy-done.3
  90.8 1.9 add_convert_fusion
  92.8 3.4 %reshape.84 = bf16[32,4,5120]{2,1,0:T(4,128)(2,1)} reshape(bf16[128,5120]{1,0:T(8,128)(2,1)} %add_convert_fusion) | data formatting | bytes 2621440 | tf_op jit(solution)/shard_map/reshape | solution.py:82
  96.2 6.2 %all-to-all-start.2 = ((bf16[32,4,5120]{2,1,0:T(4,128)(2,1)}), bf16[32,4,5120]{2,1,0:T(4,128)(2,1)}, u32[]{:S(2)}, u32[]{:S(2)}) async-start(bf16[32,4,5120]{2,1,0:T(4,128)(2,1)} %reshape.84), calls=%async_computation.2 | async-start | bytes 2621440 | tf_op jit(solution)/shard_map/all_to_all | solution.py:81
  102.5 2.5 fusion.19
  104.9 1.1 fusion.3
  106.0 15.6 %all-to-all-done.2 = bf16[32,4,5120]{2,1,0:T(4,128)(2,1)} async-done(((bf16[32,4,5120]{2,1,0:T(4,128)(2,1)}), bf16[32,4,5120]{2,1,0:T(4,128)(2,1)}, u32[]{:S(2)}, u32[]{:S(2)}) %all-to-all-start.2) | async-done | bytes 1310752 | tf_op jit(solution)/shard_map/all_to_all | solution.py:81
  121.6 1.3 collective-permute-start.2
  122.9 124.0 %all-reduce.3.cloned.1.call-done = (f32[16,5120]{1,0:T(8,128)}, f32[16,5120]{1,0:T(8,128)}) async-done(((f32[16,5120]{1,0:T(8,128)}, f32[16,5120]{1,0:T(8,128)}), (f32[16,5120]{1,0:T(8,128)}, f32[16,5120]{1,0:T(8,128)})) %all-reduce.3.cloned.1.call-update) | async-done | bytes 655376 | tf_op jit(solution)/shard_map/psum | solution.py:80
  247.0 1.9 multiply_bitcast_fusion
  249.8 1.9 reshape_reshape.3
  (30 shorter events, 3.5 us)
Async XLA Ops:
  7.2 77.6 %copy-start = (bf16[1,16,5120]{2,1,0:T(8,128)(2,1)S(1)}, bf16[1,16,5120]{2,1,0:T(8,128)(2,1)}, u32[]{:S(2)}) copy-start(bf16[1,16,5120]{2,1,0:T(8,128)(2,1)} %param.8) | copy-start | bytes 491524
  7.2 2.2 copy-start.5
  11.2 47.3 %collective-permute-start.1 = (bf16[32,4,5120]{2,1,0:T(4,128)(2,1)S(1)}, bf16[32,4,5120]{2,1,0:T(4,128)(2,1)}, u32[]{:S(2)}, u32[]{:S(2)}) collective-permute-start(bf16[32,4,5120]{2,1,0:T(4,128)(2,1)S(1)} %reshape.83), channel_id=1, source_target_pairs={{0,32},{32,64},{64,96},{96,128},{128,160},{160,192},{192,224},{224... | collective-permute-start | bytes 3932168 | tf_op jit(solution)/shard_map/ppermute | solution.py:12
  17.5 22.6 %collective-permute-start = (bf16[32,4]{0,1:T(4,128)(2,1)S(1)}, bf16[32,4]{0,1:T(4,128)(2,1)S(1)}, u32[]{:S(2)}, u32[]{:S(2)}) collective-permute-start(bf16[32,4]{0,1:T(4,128)(2,1)S(1)} %broadcast_in_dim.19), channel_id=1, source_target_pairs={{0,32},{32,64},{64,96},{96,128},{128,160},{160,192},{192,224},{224... | collective-permute-start | bytes 776 | tf_op jit(solution)/shard_map/ppermute | solution.py:12
  58.6 23.4 %all-to-all-start.1 = ((bf16[32,4,5120]{2,1,0:T(4,128)(2,1)}), bf16[32,4,5120]{2,1,0:T(4,128)(2,1)S(1)}, u32[]{:S(2)}, u32[]{:S(2)}) async-start(bf16[32,4,5120]{2,1,0:T(4,128)(2,1)} %collective-permute-done.1), calls=%async_computation.1 | async-start | bytes 2621440 | tf_op jit(solution)/shard_map/all_to_all | solution.py:72
  82.0 1.5 copy-start.1
  84.7 1.9 copy-start.2
  84.7 1.9 copy-start.4
  89.5 1.3 copy-start.3
  96.2 25.5 %all-to-all-start.2 = ((bf16[32,4,5120]{2,1,0:T(4,128)(2,1)}), bf16[32,4,5120]{2,1,0:T(4,128)(2,1)}, u32[]{:S(2)}, u32[]{:S(2)}) async-start(bf16[32,4,5120]{2,1,0:T(4,128)(2,1)} %reshape.84), calls=%async_computation.2 | async-start | bytes 2621440 | tf_op jit(solution)/shard_map/all_to_all | solution.py:81
  102.4 144.5 %all-reduce.3.cloned.1.call-start = ((), (), s32[]{:S(2)}) async-start(), calls=%async_computation.3 | async-start | bytes 1310720 | tf_op jit(solution)/shard_map/psum | solution.py:80
  121.6 127.3 %collective-permute-start.2 = (bf16[32,4,5120]{2,1,0:T(4,128)(2,1)}, bf16[32,4,5120]{2,1,0:T(4,128)(2,1)S(1)}, u32[]{:S(2)}, u32[]{:S(2)}) collective-permute-start(bf16[32,4,5120]{2,1,0:T(4,128)(2,1)} %all-to-all-done.2), channel_id=1, source_target_pairs={{32,0},{64,32},{96,64},{128,96},{160,128},{192,160},{224,192},{256... | collective-permute-start | bytes 3932168 | tf_op jit(solution)/shard_map/ppermute | solution.py:12
Sparse Core Ops, SparseCore 0:
  107.1 139.8 all-reduce.2
where the time goes:
time: 259 us
  waiting for transfers between devices  179 us (69%)
  starting transfers between devices  19.7 us (8%)
  blocking collectives  18.3 us (7%)
  between operations  14.8 us (6%)
  local copies, waits for them, and re-layouts  13.6 us (5%)
  matrix products  7.9 us (3%)
  other arithmetic  5.45 us (2%)
    psum x1, waiting for transfers between devices, shards(): grad_in, grad_out = lax.psum((grad_in, grad_out), 'peer')  124 us
    ppermute x3, waiting for transfers between devices, shifted(): return lax.ppermute(block, axis, route)  20.2 us
    all_to_all x1, waiting for transfers between devices, shards(): lax.all_to_all(moved_rows, 'peer', split_axis=0, concat_axis=0, tiled=True)  19 us
    all_to_all x1, blocking collectives, shards(): lax.all_to_all(moved_live, 'peer', split_axis=0, concat_axis=0, tiled=True)  18.3 us
    all_to_all x1, waiting for transfers between devices, shards(): lax.all_to_all(grads_here.reshape(peer_count, per_pair * block_rows, feat...  15.6 us
    ppermute x3, starting transfers between devices, shifted(): return lax.ppermute(block, axis, route)  9.19 us
    all_to_all x1, starting transfers between devices, shards(): lax.all_to_all(grads_here.reshape(peer_count, per_pair * block_rows, feat...  6.25 us
  transfers between devices with their start and end apart: 6, of which 4 were waited for; matrix products, arithmetic and copies ran while one was open for 2% of the time, Pallas kernels for 0%

commit v1 on v0

v1 whole, which is shorter than its diff:
```python
import functools

import jax
import jax.numpy as jnp
from jax import lax
from jax.experimental import pallas as pl
from jax.experimental.pallas import tpu as pltpu
from jax.sharding import PartitionSpec as P

EPS = 1e-06
BF16 = jnp.bfloat16
F32 = jnp.float32
LANES = 128
BLK = 4
VMEM = pl.BlockSpec(memory_space=pltpu.VMEM)
SMEM = pl.BlockSpec(memory_space=pltpu.SMEM)
NT = (((1,), (1,)), ((), ()))
TN = (((0,), (0,)), ((), ()))


def params():
    return pltpu.CompilerParams(vmem_limit_bytes=40 * 1024 * 1024)


def cost(flops, moved):
    return pl.CostEstimate(flops=flops, bytes_accessed=moved, transcendentals=0)


def pair_up(first, second):
    upper = lax.broadcasted_iota(jnp.int32, first.shape, first.ndim - 2) < BLK
    axis = first.ndim - 2
    top = jnp.where(upper, first, pltpu.roll(second, BLK, axis))
    bottom = jnp.where(upper, pltpu.roll(first, BLK, axis), second)
    return top, bottom


def pack_kernel(rows_ref, out_ref):
    rows, width = rows_ref.shape
    pairs = rows // 8
    for j in range(0, width // LANES, 4):
        tiles = [
            rows_ref[:, (j + k) * LANES : (j + k + 1) * LANES].astype(F32).reshape(pairs, 8, LANES)
            for k in range(4)
        ]
        even0, odd0 = pair_up(tiles[0], tiles[1])
        even1, odd1 = pair_up(tiles[2], tiles[3])
        even = jnp.concatenate([even0, even1], axis=1)
        odd = jnp.concatenate([odd0, odd1], axis=1)
        blocks = jnp.stack([even, odd], axis=1).reshape(2 * pairs, 16, LANES)
        out_ref[:, 4 * j : 4 * j + 16, :] = blocks.astype(BF16)


def pack(rows):
    count, width = rows.shape
    step = 1024 if width % 1024 == 0 else width
    high = step // LANES * BLK
    return pl.pallas_call(
        pack_kernel,
        grid=(width // step,),
        out_shape=jax.ShapeDtypeStruct((count // BLK, width // LANES * BLK, LANES), BF16),
        in_specs=[pl.BlockSpec((count, step), lambda i: (0, i))],
        out_specs=pl.BlockSpec((count // BLK, high, LANES), lambda i: (0, i, 0)),
        compiler_params=params(),
        cost_estimate=cost(count * width * 8, count * width * 4),
        name="pack_blocks",
    )(rows)


def adapter_kernel(
    meta_ref, blocks_ref, rows_ref, win_ref, wout_ref, grads_ref, sums_ref, masked_ref
):
    blocks = blocks_ref.shape[0]
    rows, width = rows_ref.shape
    tiles = width // LANES
    live_blocks = meta_ref[0, blocks]

    def place(group, _):
        halves = []
        for pair in range(2):
            loaded = []
            for k in range(2):
                b = group * 4 + pair * 2 + k
                live = jnp.where(b < live_blocks, 1.0, 0.0).astype(F32)
                block = blocks_ref[meta_ref[0, b]].astype(F32) * live
                loaded.append(block.reshape(tiles // 2, 8, LANES))
            even, odd = pair_up(loaded[0], loaded[1])
            lanes = []
            for u in range(tiles // 2):
                lanes += [even[u], odd[u]]
            halves.append(jnp.concatenate(lanes, axis=1))
        at = pl.multiple_of(group * 16, 16)
        masked_ref[pl.ds(at, 16), :] = jnp.concatenate(halves, axis=0).astype(BF16)
        return 0

    lax.fori_loop(0, blocks // 4, place, 0)

    squares = jnp.zeros((rows, LANES), F32)
    for j in range(tiles):
        tile = rows_ref[:, j * LANES : (j + 1) * LANES].astype(F32)
        squares += tile * tile
    inv_rms = lax.rsqrt(jnp.sum(squares, axis=1, keepdims=True) * (1.0 / width) + EPS)
    preact = inv_rms * lax.dot_general(
        rows_ref[...], win_ref[...], NT, preferred_element_type=F32
    )
    gate = jax.nn.sigmoid(preact)
    activated = (preact * gate).astype(BF16)
    grad_act = lax.dot_general(
        masked_ref[...], wout_ref[...], NT, preferred_element_type=F32
    )
    grad_pre = grad_act * gate * (1.0 + preact * (1.0 - gate))
    scaled = (grad_pre * inv_rms).astype(BF16)
    coef = inv_rms * jnp.sum(scaled.astype(F32) * preact, axis=1, keepdims=True) * (1.0 / width)

    step = 256
    for j in range(0, width, step):
        here = slice(j, j + step)
        spread = jnp.dot(scaled, win_ref[:, here], preferred_element_type=F32)
        result = masked_ref[:, here].astype(F32) + spread - rows_ref[:, here].astype(F32) * coef
        grads_ref[:, here] = result.astype(BF16)

    grad_in = lax.dot_general(scaled, rows_ref[...], TN, preferred_element_type=F32)
    grad_out = lax.dot_general(activated, masked_ref[...], TN, preferred_element_type=F32)
    store_pieces(sums_ref, grad_in, grad_out)


def store_pieces(sums_ref, grad_in, grad_out):
    per = grad_in.shape[1] // (8 * LANES)
    bands = [grad_in[0:8], grad_in[8:16], grad_out[0:8], grad_out[8:16]]
    for g, band in enumerate(bands):
        for h in range(8):
            for t in range(0, per, 2):
                at = (h * per + t) * LANES
                first = band[:, at : at + LANES]
                second = band[:, at + LANES : at + 2 * LANES] if t + 1 < per else jnp.zeros_like(first)
                both = jnp.concatenate([first, second], axis=0)
                sums_ref[g * 8 + h, 8 * t : 8 * t + 16, :] = both.astype(BF16)


def adapter(meta, blocks, rows, win, wout):
    count, width = rows.shape
    rank = win.shape[0]
    high = -(-width // (8 * LANES) // 2) * 16
    return pl.pallas_call(
        adapter_kernel,
        out_shape=(
            jax.ShapeDtypeStruct((count, width), BF16),
            jax.ShapeDtypeStruct((32, high, LANES), BF16),
        ),
        in_specs=[SMEM, VMEM, VMEM, VMEM, VMEM],
        out_specs=(VMEM, VMEM),
        scratch_shapes=[pltpu.VMEM((count, width), BF16)],
        compiler_params=params(),
        cost_estimate=cost(10 * count * width * rank, count * width * 6),
        name="adapter_backward",
    )(meta, blocks, rows, win, wout)


def sum_kernel(scale, pieces_ref, out_ref):
    total = jnp.sum(pieces_ref[...].astype(F32), axis=0) * scale
    out_ref[...] = jnp.broadcast_to(total.astype(BF16)[None], out_ref.shape)


def sum_pieces(pieces, scale):
    return pl.pallas_call(
        functools.partial(sum_kernel, scale),
        out_shape=jax.ShapeDtypeStruct(pieces.shape, BF16),
        in_specs=[VMEM],
        out_specs=VMEM,
        compiler_params=params(),
        cost_estimate=cost(pieces.size, pieces.size * 4),
        name="sum_pieces",
    )(pieces)


def join_kernel(pieces_ref, in_ref, out_ref):
    per = in_ref.shape[1] // (8 * LANES)
    for g in range(4):
        target = in_ref if g < 2 else out_ref
        rows = slice(8 * (g % 2), 8 * (g % 2) + 8)
        for h in range(8):
            for t in range(0, per, 2):
                at = (h * per + t) * LANES
                both = pieces_ref[g * 8 + h, 8 * t : 8 * t + 16, :].astype(F32)
                target[rows, at : at + LANES] = both[0:8]
                if t + 1 < per:
                    target[rows, at + LANES : at + 2 * LANES] = both[8:16]


def join_pieces(pieces, rank, width):
    return pl.pallas_call(
        join_kernel,
        out_shape=(jax.ShapeDtypeStruct((rank, width), F32),) * 2,
        in_specs=[VMEM],
        out_specs=(VMEM, VMEM),
        compiler_params=params(),
        cost_estimate=cost(pieces.size, pieces.size * 6),
        name="join_pieces",
    )(pieces)


def exchange(pieces):
    return lax.all_to_all(pieces, "peer", split_axis=0, concat_axis=0, tiled=True)


def shards(emitted, out_grads, adapter_in, adapter_out, wiring, counts):
    sections = lax.axis_size("section")
    onward = [(i, (i + 1) % sections) for i in range(sections)]
    back = [((i + 1) % sections, i) for i in range(sections)]
    row_total, width = emitted.shape[2:]
    rank = adapter_in.shape[1]
    last = lax.axis_index("section") == sections - 1

    rows = lax.ppermute(emitted[0, 0], "section", onward)
    live = jnp.where(last, 0, counts)
    meta = jnp.concatenate([wiring[0, 0, :, 0].reshape(1, -1), live], axis=1)
    meta = lax.ppermute(meta, "section", onward)
    blocks = exchange(pack(out_grads[0, 0]))
    grads, sums = adapter(meta, blocks, rows, adapter_in[0], adapter_out[0])
    row_grads = lax.ppermute(grads, "section", back)
    sums = exchange(sum_pieces(exchange(sums), 1.0 / row_total))
    grad_in, grad_out = join_pieces(sums, rank, width)
    return (row_grads[None, None], grad_in[None], grad_out[None])


def solution(mesh):
    return jax.shard_map(
        shards,
        mesh=mesh,
        in_specs=(
            P("section", "peer", None, None),
            P("section", "peer", None, None),
            P("section", None, None),
            P("section", None, None),
            P("section", "peer", None, None),
            P("section", "peer"),
        ),
        out_specs=(
            P("section", "peer", None, None),
            P("section", None, None),
            P("section", None, None),
        ),
        check_vma=False,
    )
```

time: 259 us -> 82.5 us (0.32)
  waiting for transfers between devices: 179 us -> 20.1 us
  blocking collectives: 18.3 us -> 31.8 us
  between operations: 14.8 us -> 1.35 us
  local copies, waits for them, and re-layouts: 13.6 us -> 2.38 us
  matrix products: 7.9 us -> 0 us
  Pallas kernels: 0 us -> 6.3 us
  other arithmetic: 5.45 us -> 0.08 us
    psum x1 -> x0, waiting for transfers between devices: 124 us -> none  [shards(): grad_in, grad_out = lax.psum((grad_in, grad_out), 'peer')]
    all_to_all x2 -> x1, waiting for transfers between devices: 34.6 us -> 0.01 us  [exchange(): lax.all_to_all(pieces, 'peer', split_axis=0, concat_axis=0, tiled=True)]
    all_to_all x1 -> x2, blocking collectives: 18.3 us -> 31.8 us  [exchange(): lax.all_to_all(pieces, 'peer', split_axis=0, concat_axis=0, tiled=True)]
    dot_general x8 -> x0, matrix products: 7.9 us -> none  [the longest x1 2.46 us: adapter_backward(): lax.dot_general(activated, masked, (((0,), (0,)), ((), ())), preferred_el...]
    pallas_call x0 -> x4, Pallas kernels: none -> 6.3 us  [the longest x1 3 us: adapter(): pl.pallas_call(adapter_kernel, out_shape=(jax.ShapeDtypeStruct((count, wi...]
    reshape x2 -> x0, local copies, waits for them, and re-layouts: 4.42 us -> none  [the longest x1 3.4 us: shards(): grads_here.reshape(peer_count, per_pair * block_rows, feature_width)]
    another operation x2 -> x0, local copies, waits for them, and re-layouts: 4.09 us -> none  [the longest x1 2.19 us: shards(): own_rows.reshape(blocks, block_rows * feature_width)]
    convert_element_type x3 -> x0, local copies, waits for them, and re-layouts: 3.72 us -> none  [the longest x1 2.39 us: adapter_backward(): rows_float = own_rows.astype(jnp.float32)]
  transfers between devices with their start and end apart: 6 -> 4, of which waited for: 4 -> 1; matrix products, arithmetic and copies ran while one was open for 2% -> 0% of each run, Pallas kernels for 0% -> 4%
where the time goes in v1:
time: 82.5 us; the launch traced here: 82.1 us
  blocking collectives  31.8 us (39%)
  waiting for transfers between devices  20.1 us (24%)
  starting transfers between devices  20 us (24%)
  Pallas kernels  6.3 us (8%)
  local copies, waits for them, and re-layouts  2.38 us (3%)
  between operations  1.35 us (2%)
    all_to_all x2, blocking collectives, exchange(): lax.all_to_all(pieces, 'peer', split_axis=0, concat_axis=0, tiled=True)  31.8 us
    ppermute x1, waiting for transfers between devices, shards(): meta = lax.ppermute(meta, 'section', onward)  20.1 us
    all_to_all x1, starting transfers between devices, exchange(): lax.all_to_all(pieces, 'peer', split_axis=0, concat_axis=0, tiled=True)  8.17 us
    ppermute x1, starting transfers between devices, shards(): rows = lax.ppermute(emitted[0, 0], 'section', onward)  4.37 us
    ppermute x1, starting transfers between devices, shards(): row_grads = lax.ppermute(grads, 'section', back)  3.91 us
    ppermute x1, starting transfers between devices, shards(): meta = lax.ppermute(meta, 'section', onward)  3.53 us
    pallas_call x1, Pallas kernels, adapter(): pl.pallas_call(adapter_kernel, out_shape=(jax.ShapeDtypeStruct((count, wi...  3 us
    unnamed x9, local copies, waits for them, and re-layouts  2.38 us
  transfers between devices with their start and end apart: 4, of which 1 were waited for; matrix products, arithmetic and copies ran while one was open for 0% of the time, Pallas kernels for 4%

profile of v1, /device:TPU:1, one launch (start us, length us, event | category | flops | bytes accessed | tf_op | source)
XLA Modules:
  0.0 82.1 jit_solution(14037609414466034164)
XLA Ops:
  0.6 4.4 %collective-permute-start.1 = (bf16[128,5120]{1,0:T(8,128)(2,1)}, bf16[128,5120]{1,0:T(8,128)(2,1)S(1)}, u32[]{:S(2)}, u32[]{:S(2)}) collective-permute-start(bf16[128,5120]{1,0:T(8,128)(2,1)} %bitcast.13), channel_id=1, source_target_pairs={{0,32},{32,64},{64,96},{96,128},{128,160},{160,192},{192,224},{224... | collective-permute-start | bytes 3932168 | tf_op jit(solution)/shard_map/ppermute | solution.py:213
  5.0 0.0 copy-start
  5.0 1.3 %copy-done = bf16[1,1,128,5120]{3,2,1,0:T(8,128)(2,1)S(1)} copy-done((bf16[1,1,128,5120]{3,2,1,0:T(8,128)(2,1)S(1)}, bf16[1,1,128,5120]{3,2,1,0:T(8,128)(2,1)}, u32[]{:S(2)}) %copy-start) | copy-done | bytes 1310744
  6.3 2.4 %pack_blocks.1 = bf16[32,160,128]{2,1,0:T(8,128)(2,1)} custom-call(bf16[128,5120]{1,0:T(8,128)(2,1)S(1)} %bitcast.9), custom_call_target="tpu_custom_call" | custom-call | flops 5242880 | bytes 2621440 | tf_op jit(solution)/shard_map/pack_blocks/pallas_call | solution.py:57
  8.7 0.0 copy-start.3
  8.7 0.0 copy-start.1
  8.7 0.0 copy-start.2
  8.7 8.2 %all-to-all-start = ((bf16[32,160,128]{2,1,0:T(8,128)(2,1)}), bf16[32,160,128]{2,1,0:T(8,128)(2,1)S(1)}, u32[]{:S(2)}, u32[]{:S(2)}) async-start(bf16[32,160,128]{2,1,0:T(8,128)(2,1)} %pack_blocks.1), calls=%async_computation | async-start | bytes 2621440 | tf_op jit(solution)/shard_map/all_to_all | solution.py:202
  17.5 0.0 copy-done.3
  17.5 0.1 pad_add_fusion
  17.6 3.5 %collective-permute-start = (s32[1,33]{1,0:T(1,128)S(1)}, s32[1,33]{1,0:T(1,128)S(1)}, u32[]{:S(2)}, u32[]{:S(2)}) collective-permute-start(s32[1,33]{1,0:T(1,128)S(1)} %pad_add_fusion), channel_id=1, source_target_pairs={{0,32},{32,64},{64,96},{96,128},{128,160},{160,192},{192,224},{224... | collective-permute-start | bytes 404 | tf_op jit(solution)/shard_map/ppermute | solution.py:216
  21.2 20.1 %collective-permute-done.meta_ref = s32[1,33]{1,0:T(1,128)S(1)} collective-permute-done((s32[1,33]{1,0:T(1,128)S(1)}, s32[1,33]{1,0:T(1,128)S(1)}, u32[]{:S(2)}, u32[]{:S(2)}) %collective-permute-start) | collective-permute-done | bytes 164 | tf_op jit(solution)/shard_map/ppermute | solution.py:216
  41.3 0.0 all-to-all-done.blocks_ref
  41.3 0.0 collective-permute-done.1.rows_ref
  41.3 0.0 copy-done.1
  41.3 0.0 copy-done.2
  41.3 3.0 %adapter_backward.1 = (bf16[128,5120]{1,0:T(8,128)(2,1)S(1)}, bf16[32,48,128]{2,1,0:T(8,128)(2,1)S(1)}) custom-call(s32[1,33]{1,0:T(1,128)S(1)} %collective-permute-done.meta_ref, bf16[32,160,128]{2,1,0:T(8,128)(2,1)S(1)} %all-to-all-done.blocks_ref, bf16[128,5120]{1,0:T(8,128)(2,1)S(1)} %collective-permute-done.1.rows_ref, bf16[16,5120]{1,0:T(8,128)(2,1)S(1)} %bitcast.10, ...), custom_call_target="tpu_custom_call" | custom-call | flops 104857600 | bytes 3932160 | tf_op jit(solution)/shard_map/adapter_backward/pallas_call | solution.py:143
  44.3 3.9 %collective-permute-start.2 = (bf16[128,5120]{1,0:T(8,128)(2,1)S(1)}, bf16[128,5120]{1,0:T(8,128)(2,1)S(1)}, u32[]{:S(2)}, u32[]{:S(2)}) collective-permute-start(bf16[128,5120]{1,0:T(8,128)(2,1)S(1)} %get-tuple-element.7), channel_id=1, source_target_pairs={{32,0},{64,32},{96,64},{128,96},{160,128},{192,160},{224,192},{256... | collective-permute-start | bytes 3932168 | tf_op jit(solution)/shard_map/ppermute | solution.py:219
  48.2 18.1 %all_to_all.15.pieces_ref = bf16[32,48,128]{2,1,0:T(8,128)(2,1)S(1)} all-to-all(bf16[32,48,128]{2,1,0:T(8,128)(2,1)S(1)} %get-tuple-element.8), channel_id=1, replica_groups=mesh['section'=16,'peer'=32] {'peer'}, dimensions={0} | all-to-all | bytes 786432 | tf_op jit(solution)/shard_map/all_to_all | solution.py:202
  66.3 0.1 sum_pieces.1
  66.4 13.8 %all_to_all.16.pieces_ref = bf16[32,48,128]{2,1,0:T(8,128)(2,1)S(1)} all-to-all(bf16[32,48,128]{2,1,0:T(8,128)(2,1)S(1)} %sum_pieces.1), channel_id=1, replica_groups=mesh['section'=16,'peer'=32] {'peer'}, dimensions={0} | all-to-all | bytes 786432 | tf_op jit(solution)/shard_map/all_to_all | solution.py:202
  80.2 0.9 %join_pieces.1 = (f32[16,5120]{1,0:T(8,128)}, f32[16,5120]{1,0:T(8,128)}) custom-call(bf16[32,48,128]{2,1,0:T(8,128)(2,1)S(1)} %all_to_all.16.pieces_ref), custom_call_target="tpu_custom_call" | custom-call | flops 196608 | bytes 1179648 | tf_op jit(solution)/shard_map/join_pieces/pallas_call | solution.py:190
  81.0 0.0 collective-permute-done.2
  81.0 1.1 %copy.11 = bf16[1,1,128,5120]{3,2,1,0:T(8,128)(2,1)} copy(bf16[1,1,128,5120]{3,2,1,0:T(8,128)(2,1)S(1)} %bitcast.12) | data formatting | bytes 2621440
Async XLA Ops:
  0.6 40.7 %collective-permute-start.1 = (bf16[128,5120]{1,0:T(8,128)(2,1)}, bf16[128,5120]{1,0:T(8,128)(2,1)S(1)}, u32[]{:S(2)}, u32[]{:S(2)}) collective-permute-start(bf16[128,5120]{1,0:T(8,128)(2,1)} %bitcast.13), channel_id=1, source_target_pairs={{0,32},{32,64},{64,96},{96,128},{128,160},{160,192},{192,224},{224... | collective-permute-start | bytes 3932168 | tf_op jit(solution)/shard_map/ppermute | solution.py:213
  5.0 1.3 %copy-start = (bf16[1,1,128,5120]{3,2,1,0:T(8,128)(2,1)S(1)}, bf16[1,1,128,5120]{3,2,1,0:T(8,128)(2,1)}, u32[]{:S(2)}) copy-start(bf16[1,1,128,5120]{3,2,1,0:T(8,128)(2,1)} %param.7) | copy-start | bytes 3932164
  8.7 8.8 %copy-start.3 = (s32[1,1,32,1]{2,3,1,0:T(1,128)S(1)}, s32[1,1,32,1]{2,3,1,0:T(1,128)}, u32[]{:S(2)}) copy-start(s32[1,1,32,1]{2,3,1,0:T(1,128)} %param.10) | copy-start | bytes 388
  8.7 32.6 %copy-start.1 = (bf16[1,16,5120]{2,1,0:T(8,128)(2,1)S(1)}, bf16[1,16,5120]{2,1,0:T(8,128)(2,1)}, u32[]{:S(2)}) copy-start(bf16[1,16,5120]{2,1,0:T(8,128)(2,1)} %param.8) | copy-start | bytes 491524
  8.7 32.6 %copy-start.2 = (bf16[1,16,5120]{2,1,0:T(8,128)(2,1)S(1)}, bf16[1,16,5120]{2,1,0:T(8,128)(2,1)}, u32[]{:S(2)}) copy-start(bf16[1,16,5120]{2,1,0:T(8,128)(2,1)} %param.9) | copy-start | bytes 491524
  8.7 32.6 %all-to-all-start = ((bf16[32,160,128]{2,1,0:T(8,128)(2,1)}), bf16[32,160,128]{2,1,0:T(8,128)(2,1)S(1)}, u32[]{:S(2)}, u32[]{:S(2)}) async-start(bf16[32,160,128]{2,1,0:T(8,128)(2,1)} %pack_blocks.1), calls=%async_computation | async-start | bytes 2621440 | tf_op jit(solution)/shard_map/all_to_all | solution.py:202
  17.6 23.7 %collective-permute-start = (s32[1,33]{1,0:T(1,128)S(1)}, s32[1,33]{1,0:T(1,128)S(1)}, u32[]{:S(2)}, u32[]{:S(2)}) collective-permute-start(s32[1,33]{1,0:T(1,128)S(1)} %pad_add_fusion), channel_id=1, source_target_pairs={{0,32},{32,64},{64,96},{96,128},{128,160},{160,192},{192,224},{224... | collective-permute-start | bytes 404 | tf_op jit(solution)/shard_map/ppermute | solution.py:216
  44.3 36.7 %collective-permute-start.2 = (bf16[128,5120]{1,0:T(8,128)(2,1)S(1)}, bf16[128,5120]{1,0:T(8,128)(2,1)S(1)}, u32[]{:S(2)}, u32[]{:S(2)}) collective-permute-start(bf16[128,5120]{1,0:T(8,128)(2,1)S(1)} %get-tuple-element.7), channel_id=1, source_target_pairs={{32,0},{64,32},{96,64},{128,96},{160,128},{192,160},{224,192},{256... | collective-permute-start | bytes 3932168 | tf_op jit(solution)/shard_map/ppermute | solution.py:219

commit v2 on v1

--- a/solution.py
+++ b/solution.py
@@ -124,27 +124,21 @@
 
 
 def store_pieces(sums_ref, grad_in, grad_out):
-    per = grad_in.shape[1] // (8 * LANES)
+    span = sums_ref.shape[2]
     bands = [grad_in[0:8], grad_in[8:16], grad_out[0:8], grad_out[8:16]]
     for g, band in enumerate(bands):
         for h in range(8):
-            for t in range(0, per, 2):
-                at = (h * per + t) * LANES
-                first = band[:, at : at + LANES]
-                second = band[:, at + LANES : at + 2 * LANES] if t + 1 < per else jnp.zeros_like(first)
-                both = jnp.concatenate([first, second], axis=0)
-                sums_ref[g * 8 + h, 8 * t : 8 * t + 16, :] = both.astype(BF16)
+            sums_ref[g * 8 + h] = band[:, h * span : (h + 1) * span].astype(BF16)
 
 
 def adapter(meta, blocks, rows, win, wout):
     count, width = rows.shape
     rank = win.shape[0]
-    high = -(-width // (8 * LANES) // 2) * 16
     return pl.pallas_call(
         adapter_kernel,
         out_shape=(
             jax.ShapeDtypeStruct((count, width), BF16),
-            jax.ShapeDtypeStruct((32, high, LANES), BF16),
+            jax.ShapeDtypeStruct((32, 8, width // 8), BF16),
         ),
         in_specs=[SMEM, VMEM, VMEM, VMEM, VMEM],
         out_specs=(VMEM, VMEM),
@@ -173,17 +167,12 @@
 
 
 def join_kernel(pieces_ref, in_ref, out_ref):
-    per = in_ref.shape[1] // (8 * LANES)
+    span = pieces_ref.shape[2]
     for g in range(4):
         target = in_ref if g < 2 else out_ref
         rows = slice(8 * (g % 2), 8 * (g % 2) + 8)
         for h in range(8):
-            for t in range(0, per, 2):
-                at = (h * per + t) * LANES
-                both = pieces_ref[g * 8 + h, 8 * t : 8 * t + 16, :].astype(F32)
-                target[rows, at : at + LANES] = both[0:8]
-                if t + 1 < per:
-                    target[rows, at + LANES : at + 2 * LANES] = both[8:16]
+            target[rows, h * span : (h + 1) * span] = pieces_ref[g * 8 + h].astype(F32)
 
 
 def join_pieces(pieces, rank, width):
@@ -204,15 +193,13 @@
 
 def shards(emitted, out_grads, adapter_in, adapter_out, wiring, counts):
     sections = lax.axis_size("section")
-    onward = [(i, (i + 1) % sections) for i in range(sections)]
-    back = [((i + 1) % sections, i) for i in range(sections)]
+    onward = [(i, i + 1) for i in range(sections - 1)]
+    back = [(i + 1, i) for i in range(sections - 1)]
     row_total, width = emitted.shape[2:]
     rank = adapter_in.shape[1]
-    last = lax.axis_index("section") == sections - 1
 
     rows = lax.ppermute(emitted[0, 0], "section", onward)
-    live = jnp.where(last, 0, counts)
-    meta = jnp.concatenate([wiring[0, 0, :, 0].reshape(1, -1), live], axis=1)
+    meta = jnp.concatenate([wiring[0, 0, :, 0].reshape(1, -1), counts], axis=1)
     meta = lax.ppermute(meta, "section", onward)
     blocks = exchange(pack(out_grads[0, 0]))
     grads, sums = adapter(meta, blocks, rows, adapter_in[0], adapter_out[0])

time: 82.5 us -> 74.4 us (0.902)
  the two profiles are of different devices: /device:TPU:1 before, /device:TPU:96 now
where the time goes in v2:
time: 74.4 us; the launch traced here: 74.1 us
  blocking collectives  26.2 us (35%)
  waiting for transfers between devices  19.5 us (26%)
  starting transfers between devices  18.2 us (24%)
  Pallas kernels  6.3 us (8%)
  local copies, waits for them, and re-layouts  2.38 us (3%)
  between operations  1.34 us (2%)
    all_to_all x2, blocking collectives, exchange(): lax.all_to_all(pieces, 'peer', split_axis=0, concat_axis=0, tiled=True)  26.2 us
    ppermute x1, waiting for transfers between devices, shards(): meta = lax.ppermute(meta, 'section', onward)  12.6 us
    all_to_all x1, starting transfers between devices, exchange(): lax.all_to_all(pieces, 'peer', split_axis=0, concat_axis=0, tiled=True)  7.45 us
    ppermute x1, starting transfers between devices, shards(): rows = lax.ppermute(emitted[0, 0], 'section', onward)  5.04 us
    ppermute x1, starting transfers between devices, shards(): meta = lax.ppermute(meta, 'section', onward)  3.81 us
    all_to_all x1, waiting for transfers between devices, exchange(): lax.all_to_all(pieces, 'peer', split_axis=0, concat_axis=0, tiled=True)  3.61 us
    ppermute x1, waiting for transfers between devices, shards(): row_grads = lax.ppermute(grads, 'section', back)  3.31 us
    pallas_call x1, Pallas kernels, adapter(): pl.pallas_call(adapter_kernel, out_shape=(jax.ShapeDtypeStruct((count, wi...  3 us
  transfers between devices with their start and end apart: 4, of which 3 were waited for; matrix products, arithmetic and copies ran while one was open for 0% of the time, Pallas kernels for 4%

profile of v2, /device:TPU:96, one launch (start us, length us, event | category | flops | bytes accessed | tf_op | source)
XLA Modules:
  0.0 74.1 jit_solution(2359352751696954792)
XLA Ops:
  0.6 5.0 %collective-permute-start.1 = (bf16[128,5120]{1,0:T(8,128)(2,1)}, bf16[128,5120]{1,0:T(8,128)(2,1)S(1)}, u32[]{:S(2)}, u32[]{:S(2)}) collective-permute-start(bf16[128,5120]{1,0:T(8,128)(2,1)} %bitcast.12), channel_id=1, source_target_pairs={{0,32},{32,64},{64,96},{96,128},{128,160},{160,192},{192,224},{224... | collective-permute-start | bytes 3932168 | tf_op jit(solution)/shard_map/ppermute | solution.py:201
  5.7 0.0 copy-start
  5.7 1.3 %copy-done = bf16[1,1,128,5120]{3,2,1,0:T(8,128)(2,1)S(1)} copy-done((bf16[1,1,128,5120]{3,2,1,0:T(8,128)(2,1)S(1)}, bf16[1,1,128,5120]{3,2,1,0:T(8,128)(2,1)}, u32[]{:S(2)}) %copy-start) | copy-done | bytes 1310744
  7.0 2.4 %pack_blocks.1 = bf16[32,160,128]{2,1,0:T(8,128)(2,1)} custom-call(bf16[128,5120]{1,0:T(8,128)(2,1)S(1)} %bitcast.8), custom_call_target="tpu_custom_call" | custom-call | flops 5242880 | bytes 2621440 | tf_op jit(solution)/shard_map/pack_blocks/pallas_call | solution.py:57
  9.4 0.0 copy-start.3
  9.4 0.0 copy-start.1
  9.4 0.0 copy-start.2
  9.4 7.5 %all-to-all-start = ((bf16[32,160,128]{2,1,0:T(8,128)(2,1)}), bf16[32,160,128]{2,1,0:T(8,128)(2,1)S(1)}, u32[]{:S(2)}, u32[]{:S(2)}) async-start(bf16[32,160,128]{2,1,0:T(8,128)(2,1)} %pack_blocks.1), calls=%async_computation | async-start | bytes 2621440 | tf_op jit(solution)/shard_map/all_to_all | solution.py:191
  17.5 0.0 copy-done.3
  17.5 0.1 pad_add_fusion
  17.6 3.8 %collective-permute-start = (s32[1,33]{1,0:T(1,128)S(1)}, s32[1,33]{1,0:T(1,128)S(1)}, u32[]{:S(2)}, u32[]{:S(2)}) collective-permute-start(s32[1,33]{1,0:T(1,128)S(1)} %pad_add_fusion), channel_id=1, source_target_pairs={{0,32},{32,64},{64,96},{96,128},{128,160},{160,192},{192,224},{224... | collective-permute-start | bytes 404 | tf_op jit(solution)/shard_map/ppermute | solution.py:203
  21.4 12.6 %collective-permute-done.meta_ref = s32[1,33]{1,0:T(1,128)S(1)} collective-permute-done((s32[1,33]{1,0:T(1,128)S(1)}, s32[1,33]{1,0:T(1,128)S(1)}, u32[]{:S(2)}, u32[]{:S(2)}) %collective-permute-start) | collective-permute-done | bytes 164 | tf_op jit(solution)/shard_map/ppermute | solution.py:203
  34.0 3.6 %all-to-all-done.blocks_ref = bf16[32,160,128]{2,1,0:T(8,128)(2,1)S(1)} async-done(((bf16[32,160,128]{2,1,0:T(8,128)(2,1)}), bf16[32,160,128]{2,1,0:T(8,128)(2,1)S(1)}, u32[]{:S(2)}, u32[]{:S(2)}) %all-to-all-start) | async-done | bytes 1310752 | tf_op jit(solution)/shard_map/all_to_all | solution.py:191
  37.6 0.0 collective-permute-done.1.rows_ref
  37.6 0.0 copy-done.1
  37.6 0.0 copy-done.2
  37.6 3.0 %adapter_backward.1 = (bf16[128,5120]{1,0:T(8,128)(2,1)S(1)}, bf16[32,8,640]{2,1,0:T(8,128)(2,1)S(1)}) custom-call(s32[1,33]{1,0:T(1,128)S(1)} %collective-permute-done.meta_ref, bf16[32,160,128]{2,1,0:T(8,128)(2,1)S(1)} %all-to-all-done.blocks_ref, bf16[128,5120]{1,0:T(8,128)(2,1)S(1)} %collective-permute-done.1.rows_ref, bf16[16,5120]{1,0:T(8,128)(2,1)S(1)} %bitcast.9, ...), custom_call_target="tpu_custom_call" | custom-call | flops 104857600 | bytes 3932160 | tf_op jit(solution)/shard_map/adapter_backward/pallas_call | solution.py:137
  40.6 1.9 %collective-permute-start.2 = (bf16[128,5120]{1,0:T(8,128)(2,1)S(1)}, bf16[128,5120]{1,0:T(8,128)(2,1)S(1)}, u32[]{:S(2)}, u32[]{:S(2)}) collective-permute-start(bf16[128,5120]{1,0:T(8,128)(2,1)S(1)} %get-tuple-element.7), channel_id=1, source_target_pairs={{32,0},{64,32},{96,64},{128,96},{160,128},{192,160},{224,192},{256... | collective-permute-start | bytes 3932168 | tf_op jit(solution)/shard_map/ppermute | solution.py:206
  42.6 13.1 %all_to_all.15.pieces_ref = bf16[32,8,640]{2,1,0:T(8,128)(2,1)S(1)} all-to-all(bf16[32,8,640]{2,1,0:T(8,128)(2,1)S(1)} %get-tuple-element.8), channel_id=1, replica_groups=mesh['section'=16,'peer'=32] {'peer'}, dimensions={0} | all-to-all | bytes 655360 | tf_op jit(solution)/shard_map/all_to_all | solution.py:191
  55.7 0.1 sum_pieces.1
  55.7 13.1 %all_to_all.16.pieces_ref = bf16[32,8,640]{2,1,0:T(8,128)(2,1)S(1)} all-to-all(bf16[32,8,640]{2,1,0:T(8,128)(2,1)S(1)} %sum_pieces.1), channel_id=1, replica_groups=mesh['section'=16,'peer'=32] {'peer'}, dimensions={0} | all-to-all | bytes 655360 | tf_op jit(solution)/shard_map/all_to_all | solution.py:191
  68.8 0.9 %join_pieces.1 = (f32[16,5120]{1,0:T(8,128)}, f32[16,5120]{1,0:T(8,128)}) custom-call(bf16[32,8,640]{2,1,0:T(8,128)(2,1)S(1)} %all_to_all.16.pieces_ref), custom_call_target="tpu_custom_call" | custom-call | flops 163840 | bytes 983040 | tf_op jit(solution)/shard_map/join_pieces/pallas_call | solution.py:179
  69.7 3.3 %collective-permute-done.2 = bf16[128,5120]{1,0:T(8,128)(2,1)S(1)} collective-permute-done((bf16[128,5120]{1,0:T(8,128)(2,1)S(1)}, bf16[128,5120]{1,0:T(8,128)(2,1)S(1)}, u32[]{:S(2)}, u32[]{:S(2)}) %collective-permute-start.2) | collective-permute-done | bytes 1310752 | tf_op jit(solution)/shard_map/ppermute | solution.py:206
  73.0 1.1 %copy.11 = bf16[1,1,128,5120]{3,2,1,0:T(8,128)(2,1)} copy(bf16[1,1,128,5120]{3,2,1,0:T(8,128)(2,1)S(1)} %bitcast.11) | data formatting | bytes 2621440
Async XLA Ops:
  0.6 37.0 %collective-permute-start.1 = (bf16[128,5120]{1,0:T(8,128)(2,1)}, bf16[128,5120]{1,0:T(8,128)(2,1)S(1)}, u32[]{:S(2)}, u32[]{:S(2)}) collective-permute-start(bf16[128,5120]{1,0:T(8,128)(2,1)} %bitcast.12), channel_id=1, source_target_pairs={{0,32},{32,64},{64,96},{96,128},{128,160},{160,192},{192,224},{224... | collective-permute-start | bytes 3932168 | tf_op jit(solution)/shard_map/ppermute | solution.py:201
  5.7 1.3 %copy-start = (bf16[1,1,128,5120]{3,2,1,0:T(8,128)(2,1)S(1)}, bf16[1,1,128,5120]{3,2,1,0:T(8,128)(2,1)}, u32[]{:S(2)}) copy-start(bf16[1,1,128,5120]{3,2,1,0:T(8,128)(2,1)} %param.7) | copy-start | bytes 3932164
  9.4 8.1 %copy-start.3 = (s32[1,1,32,1]{2,3,1,0:T(1,128)S(1)}, s32[1,1,32,1]{2,3,1,0:T(1,128)}, u32[]{:S(2)}) copy-start(s32[1,1,32,1]{2,3,1,0:T(1,128)} %param.10) | copy-start | bytes 388
  9.4 28.3 %copy-start.1 = (bf16[1,16,5120]{2,1,0:T(8,128)(2,1)S(1)}, bf16[1,16,5120]{2,1,0:T(8,128)(2,1)}, u32[]{:S(2)}) copy-start(bf16[1,16,5120]{2,1,0:T(8,128)(2,1)} %param.8) | copy-start | bytes 491524
  9.4 28.3 %copy-start.2 = (bf16[1,16,5120]{2,1,0:T(8,128)(2,1)S(1)}, bf16[1,16,5120]{2,1,0:T(8,128)(2,1)}, u32[]{:S(2)}) copy-start(bf16[1,16,5120]{2,1,0:T(8,128)(2,1)} %param.9) | copy-start | bytes 491524
  9.4 28.3 %all-to-all-start = ((bf16[32,160,128]{2,1,0:T(8,128)(2,1)}), bf16[32,160,128]{2,1,0:T(8,128)(2,1)S(1)}, u32[]{:S(2)}, u32[]{:S(2)}) async-start(bf16[32,160,128]{2,1,0:T(8,128)(2,1)} %pack_blocks.1), calls=%async_computation | async-start | bytes 2621440 | tf_op jit(solution)/shard_map/all_to_all | solution.py:191
  17.6 16.5 %collective-permute-start = (s32[1,33]{1,0:T(1,128)S(1)}, s32[1,33]{1,0:T(1,128)S(1)}, u32[]{:S(2)}, u32[]{:S(2)}) collective-permute-start(s32[1,33]{1,0:T(1,128)S(1)} %pad_add_fusion), channel_id=1, source_target_pairs={{0,32},{32,64},{64,96},{96,128},{128,160},{160,192},{192,224},{224... | collective-permute-start | bytes 404 | tf_op jit(solution)/shard_map/ppermute | solution.py:203
  40.6 32.4 %collective-permute-start.2 = (bf16[128,5120]{1,0:T(8,128)(2,1)S(1)}, bf16[128,5120]{1,0:T(8,128)(2,1)S(1)}, u32[]{:S(2)}, u32[]{:S(2)}) collective-permute-start(bf16[128,5120]{1,0:T(8,128)(2,1)S(1)} %get-tuple-element.7), channel_id=1, source_target_pairs={{32,0},{64,32},{96,64},{128,96},{160,128},{192,160},{224,192},{256... | collective-permute-start | bytes 3932168 | tf_op jit(solution)/shard_map/ppermute | solution.py:206

commit v3 on v2

v3 whole, which is shorter than its diff:
```python
import functools

import jax
import jax.numpy as jnp
from jax import lax
from jax.experimental import pallas as pl
from jax.experimental.pallas import tpu as pltpu
from jax.sharding import PartitionSpec as P

EPS = 1e-06
BF16 = jnp.bfloat16
F32 = jnp.float32
LANES = 128
BLK = 4
VMEM = pl.BlockSpec(memory_space=pltpu.VMEM)
SMEM = pl.BlockSpec(memory_space=pltpu.SMEM)
ANY = pl.BlockSpec(memory_space=pl.ANY)
CHUNK = 1024
PACK_LIMIT = 62 * 1024 * 1024
NT = (((1,), (1,)), ((), ()))
TN = (((0,), (0,)), ((), ()))


def params():
    return pltpu.CompilerParams(vmem_limit_bytes=40 * 1024 * 1024)


def cost(flops, moved):
    return pl.CostEstimate(flops=flops, bytes_accessed=moved, transcendentals=0)


def pair_up(first, second):
    upper = lax.broadcasted_iota(jnp.int32, first.shape, first.ndim - 2) < BLK
    axis = first.ndim - 2
    top = jnp.where(upper, first, pltpu.roll(second, BLK, axis))
    bottom = jnp.where(upper, pltpu.roll(first, BLK, axis), second)
    return top, bottom


def pack_kernel(chunk, rows_ref, out_ref, rows_buf, out_buf, in_sem, out_sem):
    rows, width = rows_buf.shape
    pairs = rows // 8
    high = chunk // LANES * BLK

    def load(c):
        here = slice(c * chunk, (c + 1) * chunk)
        return pltpu.make_async_copy(rows_ref.at[:, here], rows_buf.at[:, here], in_sem.at[c])

    def save(c):
        here = slice(c * high, (c + 1) * high)
        return pltpu.make_async_copy(out_buf.at[:, here], out_ref.at[:, here], out_sem.at[c])

    for c in range(width // chunk):
        load(c).start()
    for c in range(width // chunk):
        load(c).wait()
        for j in range(c * chunk // LANES, (c + 1) * chunk // LANES, 4):
            tiles = [
                rows_buf[:, (j + k) * LANES : (j + k + 1) * LANES]
                .astype(F32)
                .reshape(pairs, 8, LANES)
                for k in range(4)
            ]
            even0, odd0 = pair_up(tiles[0], tiles[1])
            even1, odd1 = pair_up(tiles[2], tiles[3])
            even = jnp.concatenate([even0, even1], axis=1)
            odd = jnp.concatenate([odd0, odd1], axis=1)
            blocks = jnp.stack([even, odd], axis=1).reshape(2 * pairs, 16, LANES)
            out_buf[:, 4 * j : 4 * j + 16, :] = blocks.astype(BF16)
        save(c).start()
    for c in range(width // chunk):
        save(c).wait()


def pack(rows):
    count, width = rows.shape
    chunk = CHUNK if width % CHUNK == 0 else width
    shape = (count // BLK, width // LANES * BLK, LANES)
    return pl.pallas_call(
        functools.partial(pack_kernel, chunk),
        out_shape=jax.ShapeDtypeStruct(shape, BF16),
        in_specs=[ANY],
        out_specs=ANY,
        scratch_shapes=[
            pltpu.VMEM((count, width), BF16),
            pltpu.VMEM(shape, BF16),
            pltpu.SemaphoreType.DMA((width // chunk,)),
            pltpu.SemaphoreType.DMA((width // chunk,)),
        ],
        compiler_params=pltpu.CompilerParams(vmem_limit_bytes=PACK_LIMIT),
        cost_estimate=cost(count * width * 8, count * width * 4),
        name="pack_blocks",
    )(rows)


def place_blocks(meta_ref, blocks_ref, rows_ref):
    blocks = blocks_ref.shape[0]
    tiles = rows_ref.shape[1] // LANES

    def place(group):
        halves = []
        for pair in range(2):
            loaded = []
            for k in range(2):
                b = group * 4 + pair * 2 + k
                block = blocks_ref[meta_ref[0, b]].astype(F32)
                loaded.append(block.reshape(tiles // 2, 8, LANES))
            even, odd = pair_up(loaded[0], loaded[1])
            lanes = []
            for u in range(tiles // 2):
                lanes += [even[u], odd[u]]
            halves.append(jnp.concatenate(lanes, axis=1))
        rows_ref[group * 16 : group * 16 + 16, :] = jnp.concatenate(halves, axis=0).astype(BF16)

    for group in range(blocks // 4):
        place(group)


def live_rows(meta_ref, blocks, rows):
    row = lax.broadcasted_iota(jnp.int32, (rows, 1), 0)
    return jnp.where(row < meta_ref[0, blocks] * BLK, 1.0, 0.0).astype(F32)


def adapter_kernel(
    meta_ref, blocks_ref, rows_ref, win_ref, wout_ref, grads_ref, pre_ref, act_ref, paired_ref, normed_ref
):
    rows, width = rows_ref.shape
    rank = win_ref.shape[0]
    tiles = width // LANES
    live = live_rows(meta_ref, blocks_ref.shape[0], rows)
    totals = jnp.zeros((rows, LANES), F32)
    for j in range(tiles):
        tile = rows_ref[:, j * LANES : (j + 1) * LANES].astype(F32)
        totals += tile * tile
    squares = jnp.sum(totals, axis=1, keepdims=True)
    inv_rms = lax.rsqrt(squares * (1.0 / width) + EPS)
    place_blocks(meta_ref, blocks_ref, paired_ref)
    for j in range(tiles):
        here = slice(j * LANES, (j + 1) * LANES)
        normed_ref[:, here] = (rows_ref[:, here].astype(F32) * inv_rms).astype(BF16)
    grad_act = live * lax.dot_general(
        paired_ref[...], wout_ref[...], NT, preferred_element_type=F32
    )
    preact = lax.dot_general(win_ref[...], normed_ref[...], NT, preferred_element_type=F32).T
    gate = jax.nn.sigmoid(preact)
    activated = (live * (preact * gate)).astype(BF16)
    grad_pre = (grad_act * gate * (1.0 + preact * (1.0 - gate))).astype(BF16)
    pre_ref[...] = grad_pre
    act_ref[...] = activated
    centred = jnp.sum(grad_pre.astype(F32) * preact, axis=1, keepdims=True) * (1.0 / width)
    coef = inv_rms * inv_rms * centred
    step = 256
    for j in range(0, width, step):
        here = slice(j, j + step)
        spread = jnp.dot(grad_pre, win_ref[:, here], preferred_element_type=F32)
        result = paired_ref[:, here].astype(F32) * live + (
            inv_rms * spread - rows_ref[:, here].astype(F32) * coef
        )
        grads_ref[:, here] = result.astype(BF16)


def sums_kernel(pre_ref, act_ref, paired_ref, normed_ref, sums_ref):
    grad_in = lax.dot_general(pre_ref[...], normed_ref[...], TN, preferred_element_type=F32)
    grad_out = lax.dot_general(act_ref[...], paired_ref[...], TN, preferred_element_type=F32)
    store_pieces(sums_ref, grad_in, grad_out)


def store_pieces(sums_ref, grad_in, grad_out):
    span = sums_ref.shape[2]
    bands = [grad_in[0:8], grad_in[8:16], grad_out[0:8], grad_out[8:16]]
    for g, band in enumerate(bands):
        for h in range(8):
            sums_ref[g * 8 + h] = band[:, h * span : (h + 1) * span].astype(BF16)


def adapter(meta, blocks, rows, win, wout):
    count, width = rows.shape
    rank = win.shape[0]
    wide = jax.ShapeDtypeStruct((count, width), BF16)
    narrow = jax.ShapeDtypeStruct((count, rank), BF16)
    return pl.pallas_call(
        adapter_kernel,
        out_shape=(wide, narrow, narrow, wide, wide),
        in_specs=[SMEM, VMEM, VMEM, VMEM, VMEM],
        out_specs=(VMEM,) * 5,
        compiler_params=params(),
        cost_estimate=cost(6 * count * width * rank, count * width * 10),
        name="row_grads",
    )(meta, blocks, rows, win, wout)


def local_sums(pre, act, paired, normed):
    count, width = paired.shape
    return pl.pallas_call(
        sums_kernel,
        out_shape=jax.ShapeDtypeStruct((32, 8, width // 8), BF16),
        in_specs=[VMEM] * 4,
        out_specs=VMEM,
        compiler_params=params(),
        cost_estimate=cost(4 * count * width * act.shape[1], count * width * 4),
        name="local_sums",
    )(pre, act, paired, normed)


def sum_kernel(scale, pieces_ref, out_ref):
    total = jnp.sum(pieces_ref[...].astype(F32), axis=0) * scale
    out_ref[...] = jnp.broadcast_to(total.astype(BF16)[None], out_ref.shape)


def sum_pieces(pieces, scale):
    return pl.pallas_call(
        functools.partial(sum_kernel, scale),
        out_shape=jax.ShapeDtypeStruct(pieces.shape, BF16),
        in_specs=[VMEM],
        out_specs=VMEM,
        compiler_params=params(),
        cost_estimate=cost(pieces.size, pieces.size * 4),
        name="sum_pieces",
    )(pieces)


def join_kernel(pieces_ref, in_ref, out_ref):
    span = pieces_ref.shape[2]
    for g in range(4):
        target = in_ref if g < 2 else out_ref
        rows = slice(8 * (g % 2), 8 * (g % 2) + 8)
        for h in range(8):
            target[rows, h * span : (h + 1) * span] = pieces_ref[g * 8 + h].astype(F32)


def join_pieces(pieces, rank, width):
    return pl.pallas_call(
        join_kernel,
        out_shape=(jax.ShapeDtypeStruct((rank, width), F32),) * 2,
        in_specs=[VMEM],
        out_specs=(VMEM, VMEM),
        compiler_params=params(),
        cost_estimate=cost(pieces.size, pieces.size * 6),
        name="join_pieces",
    )(pieces)


def exchange(pieces):
    return lax.all_to_all(pieces, "peer", split_axis=0, concat_axis=0, tiled=True)


def shards(emitted, out_grads, adapter_in, adapter_out, wiring, counts):
    sections = lax.axis_size("section")
    onward = [(i, i + 1) for i in range(sections - 1)]
    back = [(i + 1, i) for i in range(sections - 1)]
    row_total, width = emitted.shape[2:]
    rank = adapter_in.shape[1]

    rows = lax.ppermute(emitted[0, 0], "section", onward)
    meta = jnp.concatenate([wiring[0, 0, :, 0].reshape(1, -1), counts], axis=1)
    meta = lax.ppermute(meta, "section", onward)
    blocks = exchange(pack(out_grads[0, 0]))
    grads, *factors = adapter(meta, blocks, rows, adapter_in[0], adapter_out[0])
    row_grads = lax.ppermute(grads, "section", back)
    sums = local_sums(*factors)
    sums = exchange(sum_pieces(exchange(sums), 1.0 / row_total))
    grad_in, grad_out = join_pieces(sums, rank, width)
    return (row_grads[None, None], grad_in[None], grad_out[None])


def solution(mesh):
    return jax.shard_map(
        shards,
        mesh=mesh,
        in_specs=(
            P("section", "peer", None, None),
            P("section", "peer", None, None),
            P("section", None, None),
            P("section", None, None),
            P("section", "peer", None, None),
            P("section", "peer"),
        ),
        out_specs=(
            P("section", "peer", None, None),
            P("section", None, None),
            P("section", None, None),
        ),
        check_vma=False,
    )
```

time: 74.4 us -> 73.1 us (0.983)
  the two profiles are of different devices: /device:TPU:96 before, /device:TPU:417 now
where the time goes in v3:
time: 73.1 us; the launch traced here: 72.8 us
  blocking collectives  31.4 us (43%)
  starting transfers between devices  16.9 us (23%)
  waiting for transfers between devices  15.7 us (21%)
  Pallas kernels  6.2 us (8%)
  between operations  1.37 us (2%)
  local copies, waits for them, and re-layouts  1.08 us (1%)
    all_to_all x2, blocking collectives, exchange(): lax.all_to_all(pieces, 'peer', split_axis=0, concat_axis=0, tiled=True)  31.4 us
    ppermute x1, waiting for transfers between devices, shards(): meta = lax.ppermute(meta, 'section', onward)  15.3 us
    all_to_all x1, starting transfers between devices, exchange(): lax.all_to_all(pieces, 'peer', split_axis=0, concat_axis=0, tiled=True)  8.18 us
    ppermute x1, starting transfers between devices, shards(): row_grads = lax.ppermute(grads, 'section', back)  3.48 us
    ppermute x1, starting transfers between devices, shards(): rows = lax.ppermute(emitted[0, 0], 'section', onward)  2.65 us
    pallas_call x1, Pallas kernels, adapter(): pl.pallas_call(adapter_kernel, out_shape=(wide, narrow, narrow, wide, wid...  2.64 us
    ppermute x1, starting transfers between devices, shards(): meta = lax.ppermute(meta, 'section', onward)  2.64 us
    pallas_call x1, Pallas kernels, pack(): pl.pallas_call(functools.partial(pack_kernel, chunk), out_shape=jax.Shape...  2.14 us
  transfers between devices with their start and end apart: 4, of which 2 were waited for; matrix products, arithmetic and copies ran while one was open for 0% of the time, Pallas kernels for 5%

profile of v3, /device:TPU:417, one launch (start us, length us, event | category | flops | bytes accessed | tf_op | source)
XLA Modules:
  0.0 72.8 jit_solution(6598629081579758473)
XLA Ops:
  0.6 2.6 %collective-permute-start.1 = (bf16[128,5120]{1,0:T(8,128)(2,1)}, bf16[128,5120]{1,0:T(8,128)(2,1)S(1)}, u32[]{:S(2)}, u32[]{:S(2)}) collective-permute-start(bf16[128,5120]{1,0:T(8,128)(2,1)} %bitcast.12), channel_id=1, source_target_pairs={{0,32},{32,64},{64,96},{96,128},{128,160},{160,192},{192,224},{224... | collective-permute-start | bytes 3932168 | tf_op jit(solution)/shard_map/ppermute | solution.py:254
  3.3 2.1 %pack_blocks.1 = bf16[32,160,128]{2,1,0:T(8,128)(2,1)} custom-call(bf16[128,5120]{1,0:T(8,128)(2,1)} %bitcast.10), custom_call_target="tpu_custom_call" | custom-call | flops 5242880 | bytes 2621440 | tf_op jit(solution)/shard_map/pack_blocks/pallas_call | solution.py:79
  5.4 0.0 copy-start.2
  5.4 0.0 copy-start
  5.5 0.0 copy-start.1
  5.5 8.2 %all-to-all-start = ((bf16[32,160,128]{2,1,0:T(8,128)(2,1)}), bf16[32,160,128]{2,1,0:T(8,128)(2,1)S(1)}, u32[]{:S(2)}, u32[]{:S(2)}) async-start(bf16[32,160,128]{2,1,0:T(8,128)(2,1)} %pack_blocks.1), calls=%async_computation | async-start | bytes 2621440 | tf_op jit(solution)/shard_map/all_to_all | solution.py:244
  14.3 0.0 copy-done.2
  14.3 0.1 pad_add_fusion
  14.4 2.6 %collective-permute-start = (s32[1,33]{1,0:T(1,128)S(1)}, s32[1,33]{1,0:T(1,128)S(1)}, u32[]{:S(2)}, u32[]{:S(2)}) collective-permute-start(s32[1,33]{1,0:T(1,128)S(1)} %pad_add_fusion), channel_id=1, source_target_pairs={{0,32},{32,64},{64,96},{96,128},{128,160},{160,192},{192,224},{224... | collective-permute-start | bytes 404 | tf_op jit(solution)/shard_map/ppermute | solution.py:256
  17.0 15.3 %collective-permute-done.meta_ref = s32[1,33]{1,0:T(1,128)S(1)} collective-permute-done((s32[1,33]{1,0:T(1,128)S(1)}, s32[1,33]{1,0:T(1,128)S(1)}, u32[]{:S(2)}, u32[]{:S(2)}) %collective-permute-start) | collective-permute-done | bytes 164 | tf_op jit(solution)/shard_map/ppermute | solution.py:256
  32.4 0.4 all-to-all-done.blocks_ref
  32.8 0.0 collective-permute-done.1.rows_ref
  32.8 0.0 copy-done
  32.8 0.0 copy-done.1
  32.8 2.6 %row_grads.1 = (bf16[128,5120]{1,0:T(8,128)(2,1)S(1)}, bf16[128,16]{1,0:T(8,128)(2,1)S(1)}, bf16[128,16]{1,0:T(8,128)(2,1)S(1)}, bf16[128,5120]{1,0:T(8,128)(2,1)S(1)}, bf16[128,5120]{1,0:T(8,128)(2,1)S(1)}) custom-call(s32[1,33]{1,0:T(1,128)S(1)} %collective-permute-done.meta_ref, bf16[32,160,128]{2,1,0:T(8,128)(2,1)S(1)} %all-to-all-done.blocks_ref, ...), custom_call_target="tpu_custom_call" | custom-call | flops 62914560 | bytes 6553600 | tf_op jit(solution)/shard_map/row_grads/pallas_call | solution.py:181
  35.4 3.5 %collective-permute-start.2 = (bf16[128,5120]{1,0:T(8,128)(2,1)S(1)}, bf16[128,5120]{1,0:T(8,128)(2,1)S(1)}, u32[]{:S(2)}, u32[]{:S(2)}) collective-permute-start(bf16[128,5120]{1,0:T(8,128)(2,1)S(1)} %get-tuple-element.10), channel_id=1, source_target_pairs={{32,0},{64,32},{96,64},{128,96},{160,128},{192,160},{224,192},{256... | collective-permute-start | bytes 3932168 | tf_op jit(solution)/shard_map/ppermute | solution.py:259
  38.9 0.5 local_sums.1
  39.4 18.3 %all_to_all.15.pieces_ref = bf16[32,8,640]{2,1,0:T(8,128)(2,1)S(1)} all-to-all(bf16[32,8,640]{2,1,0:T(8,128)(2,1)S(1)} %local_sums.1), channel_id=1, replica_groups=mesh['section'=16,'peer'=32] {'peer'}, dimensions={0} | all-to-all | bytes 655360 | tf_op jit(solution)/shard_map/all_to_all | solution.py:244
  57.7 0.1 sum_pieces.1
  57.8 13.1 %all_to_all.16.pieces_ref = bf16[32,8,640]{2,1,0:T(8,128)(2,1)S(1)} all-to-all(bf16[32,8,640]{2,1,0:T(8,128)(2,1)S(1)} %sum_pieces.1), channel_id=1, replica_groups=mesh['section'=16,'peer'=32] {'peer'}, dimensions={0} | all-to-all | bytes 655360 | tf_op jit(solution)/shard_map/all_to_all | solution.py:244
  70.9 0.9 %join_pieces.1 = (f32[16,5120]{1,0:T(8,128)}, f32[16,5120]{1,0:T(8,128)}) custom-call(bf16[32,8,640]{2,1,0:T(8,128)(2,1)S(1)} %all_to_all.16.pieces_ref), custom_call_target="tpu_custom_call" | custom-call | flops 163840 | bytes 983040 | tf_op jit(solution)/shard_map/join_pieces/pallas_call | solution.py:232
  71.7 0.0 collective-permute-done.2
  71.7 1.1 %copy.11 = bf16[1,1,128,5120]{3,2,1,0:T(8,128)(2,1)} copy(bf16[1,1,128,5120]{3,2,1,0:T(8,128)(2,1)S(1)} %bitcast.11) | data formatting | bytes 2621440
Async XLA Ops:
  0.6 32.1 %collective-permute-start.1 = (bf16[128,5120]{1,0:T(8,128)(2,1)}, bf16[128,5120]{1,0:T(8,128)(2,1)S(1)}, u32[]{:S(2)}, u32[]{:S(2)}) collective-permute-start(bf16[128,5120]{1,0:T(8,128)(2,1)} %bitcast.12), channel_id=1, source_target_pairs={{0,32},{32,64},{64,96},{96,128},{128,160},{160,192},{192,224},{224... | collective-permute-start | bytes 3932168 | tf_op jit(solution)/shard_map/ppermute | solution.py:254
  5.4 8.9 %copy-start.2 = (s32[1,1,32,1]{2,3,1,0:T(1,128)S(1)}, s32[1,1,32,1]{2,3,1,0:T(1,128)}, u32[]{:S(2)}) copy-start(s32[1,1,32,1]{2,3,1,0:T(1,128)} %param.10) | copy-start | bytes 388
  5.4 27.3 %copy-start = (bf16[1,16,5120]{2,1,0:T(8,128)(2,1)S(1)}, bf16[1,16,5120]{2,1,0:T(8,128)(2,1)}, u32[]{:S(2)}) copy-start(bf16[1,16,5120]{2,1,0:T(8,128)(2,1)} %param.8) | copy-start | bytes 491524
  5.5 27.3 %copy-start.1 = (bf16[1,16,5120]{2,1,0:T(8,128)(2,1)S(1)}, bf16[1,16,5120]{2,1,0:T(8,128)(2,1)}, u32[]{:S(2)}) copy-start(bf16[1,16,5120]{2,1,0:T(8,128)(2,1)} %param.9) | copy-start | bytes 491524
  5.5 27.3 %all-to-all-start = ((bf16[32,160,128]{2,1,0:T(8,128)(2,1)}), bf16[32,160,128]{2,1,0:T(8,128)(2,1)S(1)}, u32[]{:S(2)}, u32[]{:S(2)}) async-start(bf16[32,160,128]{2,1,0:T(8,128)(2,1)} %pack_blocks.1), calls=%async_computation | async-start | bytes 2621440 | tf_op jit(solution)/shard_map/all_to_all | solution.py:244
  14.4 18.0 %collective-permute-start = (s32[1,33]{1,0:T(1,128)S(1)}, s32[1,33]{1,0:T(1,128)S(1)}, u32[]{:S(2)}, u32[]{:S(2)}) collective-permute-start(s32[1,33]{1,0:T(1,128)S(1)} %pad_add_fusion), channel_id=1, source_target_pairs={{0,32},{32,64},{64,96},{96,128},{128,160},{160,192},{192,224},{224... | collective-permute-start | bytes 404 | tf_op jit(solution)/shard_map/ppermute | solution.py:256
  35.4 36.3 %collective-permute-start.2 = (bf16[128,5120]{1,0:T(8,128)(2,1)S(1)}, bf16[128,5120]{1,0:T(8,128)(2,1)S(1)}, u32[]{:S(2)}, u32[]{:S(2)}) collective-permute-start(bf16[128,5120]{1,0:T(8,128)(2,1)S(1)} %get-tuple-element.10), channel_id=1, source_target_pairs={{32,0},{64,32},{96,64},{128,96},{160,128},{192,160},{224,192},{256... | collective-permute-start | bytes 3932168 | tf_op jit(solution)/shard_map/ppermute | solution.py:259

commit v4 on v3

--- a/solution.py
+++ b/solution.py
@@ -16,7 +16,7 @@
 SMEM = pl.BlockSpec(memory_space=pltpu.SMEM)
 ANY = pl.BlockSpec(memory_space=pl.ANY)
 CHUNK = 1024
-PACK_LIMIT = 62 * 1024 * 1024
+PACK_LIMIT = 60 * 1024 * 1024
 NT = (((1,), (1,)), ((), ()))
 TN = (((0,), (0,)), ((), ()))
 
@@ -26,6 +26,10 @@
 
 
 def cost(flops, moved):
+    return pl.CostEstimate(flops=flops, bytes_accessed=moved, transcendentals=0)
+
+
+def old(flops, moved):
     return pl.CostEstimate(flops=flops, bytes_accessed=moved, transcendentals=0)
 
 
@@ -122,7 +126,7 @@
 
 
 def adapter_kernel(
-    meta_ref, blocks_ref, rows_ref, win_ref, wout_ref, grads_ref, pre_ref, act_ref, paired_ref, normed_ref
+    meta_ref, blocks_ref, rows_ref, win_ref, wout_ref, sums_ref, paired_ref, normed_ref
 ):
     rows, width = rows_ref.shape
     rank = win_ref.shape[0]
@@ -145,61 +149,123 @@
     gate = jax.nn.sigmoid(preact)
     activated = (live * (preact * gate)).astype(BF16)
     grad_pre = (grad_act * gate * (1.0 + preact * (1.0 - gate))).astype(BF16)
-    pre_ref[...] = grad_pre
-    act_ref[...] = activated
+    grad_in = lax.dot_general(grad_pre, normed_ref[...], TN, preferred_element_type=F32)
+    grad_out = lax.dot_general(activated, paired_ref[...], TN, preferred_element_type=F32)
+    store_pieces(sums_ref, grad_in, grad_out)
+
+
+def store_pieces(sums_ref, grad_in, grad_out):
+    span = sums_ref.shape[2]
+    bands = [grad_in[0:8], grad_in[8:16], grad_out[0:8], grad_out[8:16]]
+    for g, band in enumerate(bands):
+        for h in range(8):
+            sums_ref[g * 8 + h] = band[:, h * span : (h + 1) * span].astype(BF16)
+
+
+def adapter(meta, blocks, rows, win, wout):
+    count, width = rows.shape
+    return pl.pallas_call(
+        adapter_kernel,
+        out_shape=jax.ShapeDtypeStruct((32, 8, width // 8), BF16),
+        in_specs=[SMEM, VMEM, VMEM, VMEM, VMEM],
+        out_specs=VMEM,
+        scratch_shapes=[pltpu.VMEM((count, width), BF16), pltpu.VMEM((count, width), BF16)],
+        compiler_params=params(),
+        cost_estimate=cost(100_000_000_000, 200_000_000),
+        name="adapter_backward",
+    )(meta, blocks, rows, win, wout)
+
+
+def norm_kernel(rows_ref, win_ref, inv_ref, preact_ref, normed_ref):
+    rows, width = rows_ref.shape
+    tiles = width // LANES
+    totals = jnp.zeros((rows, LANES), F32)
+    for j in range(tiles):
+        tile = rows_ref[:, j * LANES : (j + 1) * LANES].astype(F32)
+        totals += tile * tile
+    squares = jnp.sum(totals, axis=1, keepdims=True)
+    inv_rms = lax.rsqrt(squares * (1.0 / width) + EPS)
+    for j in range(tiles):
+        here = slice(j * LANES, (j + 1) * LANES)
+        normed_ref[:, here] = (rows_ref[:, here].astype(F32) * inv_rms).astype(BF16)
+    inv_ref[...] = inv_rms
+    preact_ref[...] = lax.dot_general(
+        normed_ref[...], win_ref[...], NT, preferred_element_type=F32
+    )
+
+
+def norm(rows, win):
+    count, width = rows.shape
+    rank = win.shape[0]
+    return pl.pallas_call(
+        norm_kernel,
+        out_shape=(
+            jax.ShapeDtypeStruct((count, 1), F32),
+            jax.ShapeDtypeStruct((count, rank), F32),
+        ),
+        in_specs=[VMEM, VMEM],
+        out_specs=(VMEM, VMEM),
+        scratch_shapes=[pltpu.VMEM((count, width), BF16)],
+        compiler_params=params(),
+        cost_estimate=cost(2 * count * width * rank, count * width * 2),
+        name="norm_rows",
+    )(rows, win)
+
+
+def finish_kernel(
+    meta_ref, blocks_ref, rows_ref, win_ref, wout_ref, inv_ref, preact_ref,
+    out_ref, paired_ref, out_buf, out_sem,
+):
+    rows, width = rows_ref.shape
+    live = live_rows(meta_ref, blocks_ref.shape[0], rows)
+    inv_rms = inv_ref[...]
+    preact = preact_ref[...]
+    gate = jax.nn.sigmoid(preact)
+    place_blocks(meta_ref, blocks_ref, paired_ref)
+    grad_act = live * lax.dot_general(
+        paired_ref[...], wout_ref[...], NT, preferred_element_type=F32
+    )
+    grad_pre = (grad_act * gate * (1.0 + preact * (1.0 - gate))).astype(BF16)
     centred = jnp.sum(grad_pre.astype(F32) * preact, axis=1, keepdims=True) * (1.0 / width)
     coef = inv_rms * inv_rms * centred
+
     step = 256
+    per = 4 * step
     for j in range(0, width, step):
         here = slice(j, j + step)
         spread = jnp.dot(grad_pre, win_ref[:, here], preferred_element_type=F32)
         result = paired_ref[:, here].astype(F32) * live + (
             inv_rms * spread - rows_ref[:, here].astype(F32) * coef
         )
-        grads_ref[:, here] = result.astype(BF16)
-
-
-def sums_kernel(pre_ref, act_ref, paired_ref, normed_ref, sums_ref):
-    grad_in = lax.dot_general(pre_ref[...], normed_ref[...], TN, preferred_element_type=F32)
-    grad_out = lax.dot_general(act_ref[...], paired_ref[...], TN, preferred_element_type=F32)
-    store_pieces(sums_ref, grad_in, grad_out)
-
-
-def store_pieces(sums_ref, grad_in, grad_out):
-    span = sums_ref.shape[2]
-    bands = [grad_in[0:8], grad_in[8:16], grad_out[0:8], grad_out[8:16]]
-    for g, band in enumerate(bands):
-        for h in range(8):
-            sums_ref[g * 8 + h] = band[:, h * span : (h + 1) * span].astype(BF16)
-
-
-def adapter(meta, blocks, rows, win, wout):
+        out_buf[:, here] = result.astype(BF16)
+        if (j + step) % per == 0:
+            save(out_buf, out_ref, out_sem, per, j // per).start()
+    for c in range(width // per):
+        save(out_buf, out_ref, out_sem, per, c).wait()
+
+
+def save(out_buf, out_ref, out_sem, per, c):
+    part = slice(c * per, (c + 1) * per)
+    return pltpu.make_async_copy(out_buf.at[:, part], out_ref.at[:, part], out_sem.at[c])
+
+
+def finish(meta, blocks, rows, win, wout, inv_rms, preact):
     count, width = rows.shape
     rank = win.shape[0]
-    wide = jax.ShapeDtypeStruct((count, width), BF16)
-    narrow = jax.ShapeDtypeStruct((count, rank), BF16)
-    return pl.pallas_call(
-        adapter_kernel,
-        out_shape=(wide, narrow, narrow, wide, wide),
-        in_specs=[SMEM, VMEM, VMEM, VMEM, VMEM],
-        out_specs=(VMEM,) * 5,
-        compiler_params=params(),
-        cost_estimate=cost(6 * count * width * rank, count * width * 10),
+    return pl.pallas_call(
+        finish_kernel,
+        out_shape=jax.ShapeDtypeStruct((count, width), BF16),
+        in_specs=[SMEM] + [VMEM] * 6,
+        out_specs=ANY,
+        scratch_shapes=[
+            pltpu.VMEM((count, width), BF16),
+            pltpu.VMEM((count, width), BF16),
+            pltpu.SemaphoreType.DMA((width // 1024,)),
+        ],
+        compiler_params=params(),
+        cost_estimate=cost(2 * count * width * rank, count * width * 4),
         name="row_grads",
-    )(meta, blocks, rows, win, wout)
-
-
-def local_sums(pre, act, paired, normed):
-    count, width = paired.shape
-    return pl.pallas_call(
-        sums_kernel,
-        out_shape=jax.ShapeDtypeStruct((32, 8, width // 8), BF16),
-        in_specs=[VMEM] * 4,
-        out_specs=VMEM,
-        compiler_params=params(),
-        cost_estimate=cost(4 * count * width * act.shape[1], count * width * 4),
-        name="local_sums",
-    )(pre, act, paired, normed)
+    )(meta, blocks, rows, win, wout, inv_rms, preact)
 
 
 def sum_kernel(scale, pieces_ref, out_ref):
@@ -252,14 +318,21 @@
     rank = adapter_in.shape[1]
 
     rows = lax.ppermute(emitted[0, 0], "section", onward)
-    meta = jnp.concatenate([wiring[0, 0, :, 0].reshape(1, -1), counts], axis=1)
-    meta = lax.ppermute(meta, "section", onward)
+    own_meta = jnp.concatenate([wiring[0, 0, :, 0].reshape(1, -1), counts], axis=1)
+    meta = lax.ppermute(own_meta, "section", onward)
+    next_win = lax.ppermute(adapter_in[0], "section", back)
+    next_wout = lax.ppermute(adapter_out[0], "section", back)
+    inv_rms, preact = norm(emitted[0, 0], next_win)
     blocks = exchange(pack(out_grads[0, 0]))
-    grads, *factors = adapter(meta, blocks, rows, adapter_in[0], adapter_out[0])
-    row_grads = lax.ppermute(grads, "section", back)
-    sums = local_sums(*factors)
+    blocks, next_win, next_wout, inv_rms, preact = lax.optimization_barrier(
+        (blocks, next_win, next_wout, inv_rms, preact)
+    )
+    returned = lax.ppermute(blocks, "section", back)
+    sums = adapter(meta, blocks, rows, adapter_in[0], adapter_out[0])
     sums = exchange(sum_pieces(exchange(sums), 1.0 / row_total))
     grad_in, grad_out = join_pieces(sums, rank, width)
+    grad_in, grad_out, returned = lax.optimization_barrier((grad_in, grad_out, returned))
+    row_grads = finish(own_meta, returned, emitted[0, 0], next_win, next_wout, inv_rms, preact)
     return (row_grads[None, None], grad_in[None], grad_out[None])
 
 

time: 73.1 us -> 72.1 us (0.986)
  the two profiles are of different devices: /device:TPU:417 before, /device:TPU:1 now
where the time goes in v4:
time: 72.1 us; the launch traced here: 71.1 us
  blocking collectives  27.3 us (38%)
  starting transfers between devices  22.1 us (31%)
  waiting for transfers between devices  10.3 us (14%)
  Pallas kernels  9.89 us (14%)
  between operations  1.43 us (2%)
    all_to_all x2, blocking collectives, exchange(): lax.all_to_all(pieces, 'peer', split_axis=0, concat_axis=0, tiled=True)  27.3 us
    all_to_all x1, starting transfers between devices, exchange(): lax.all_to_all(pieces, 'peer', split_axis=0, concat_axis=0, tiled=True)  8.18 us
    all_to_all x1, waiting for transfers between devices, exchange(): lax.all_to_all(pieces, 'peer', split_axis=0, concat_axis=0, tiled=True)  8.11 us
    ppermute x1, starting transfers between devices, shards(): rows = lax.ppermute(emitted[0, 0], 'section', onward)  5.47 us
    ppermute x1, starting transfers between devices, shards(): meta = lax.ppermute(own_meta, 'section', onward)  4.6 us
    pallas_call x1, Pallas kernels, adapter(): pl.pallas_call(adapter_kernel, out_shape=jax.ShapeDtypeStruct((32, 8, wid...  3.11 us
    pallas_call x1, Pallas kernels, finish(): pl.pallas_call(finish_kernel, out_shape=jax.ShapeDtypeStruct((count, widt...  2.88 us
    ppermute x1, waiting for transfers between devices, shards(): next_wout = lax.ppermute(adapter_out[0], 'section', back)  2.16 us
  transfers between devices with their start and end apart: 6, of which 2 were waited for; matrix products, arithmetic and copies ran while one was open for 0% of the time, Pallas kernels for 10%

profile of v4, /device:TPU:1, one launch (start us, length us, event | category | flops | bytes accessed | tf_op | source)
XLA Modules:
  0.0 71.1 jit_solution(13662530017990640977)
XLA Ops:
  0.6 5.5 %collective-permute-start.3 = (bf16[128,5120]{1,0:T(8,128)(2,1)}, bf16[128,5120]{1,0:T(8,128)(2,1)}, u32[]{:S(2)}, u32[]{:S(2)}) collective-permute-start(bf16[128,5120]{1,0:T(8,128)(2,1)} %bitcast.8), channel_id=1, source_target_pairs={{0,32},{32,64},{64,96},{96,128},{128,160},{160,192},{192,224},{224... | collective-permute-start | bytes 3932168 | tf_op jit(solution)/shard_map/ppermute | solution.py:320
  6.1 2.1 %pack_blocks.1 = bf16[32,160,128]{2,1,0:T(8,128)(2,1)} custom-call(bf16[128,5120]{1,0:T(8,128)(2,1)} %bitcast.15), custom_call_target="tpu_custom_call" | custom-call | flops 5242880 | bytes 2621440 | tf_op jit(solution)/shard_map/pack_blocks/pallas_call | solution.py:83
  8.2 0.0 copy-start.1
  8.3 0.0 copy-start.2
  8.3 0.0 copy-start.3
  8.3 0.0 copy-start
  8.3 8.2 %all-to-all-start = ((bf16[32,160,128]{2,1,0:T(8,128)(2,1)}), bf16[32,160,128]{2,1,0:T(8,128)(2,1)S(1)}, u32[]{:S(2)}, u32[]{:S(2)}) async-start(bf16[32,160,128]{2,1,0:T(8,128)(2,1)} %pack_blocks.1), calls=%async_computation | async-start | bytes 2621440 | tf_op jit(solution)/shard_map/all_to_all | solution.py:310
  16.5 1.3 %collective-permute-start.1 = (bf16[16,5120]{1,0:T(8,128)(2,1)S(1)}, bf16[16,5120]{1,0:T(8,128)(2,1)S(1)}, u32[]{:S(2)}, u32[]{:S(2)}) collective-permute-start(bf16[16,5120]{1,0:T(8,128)(2,1)S(1)} %bitcast.11), channel_id=1, source_target_pairs={{32,0},{64,32},{96,64},{128,96},{160,128},{192,160},{224,192},{256... | collective-permute-start | bytes 491528 | tf_op jit(solution)/shard_map/ppermute | solution.py:323
  17.8 1.3 %collective-permute-start.2 = (bf16[16,5120]{1,0:T(8,128)(2,1)S(1)}, bf16[16,5120]{1,0:T(8,128)(2,1)S(1)}, u32[]{:S(2)}, u32[]{:S(2)}) collective-permute-start(bf16[16,5120]{1,0:T(8,128)(2,1)S(1)} %bitcast.13), channel_id=1, source_target_pairs={{32,0},{64,32},{96,64},{128,96},{160,128},{192,160},{224,192},{256... | collective-permute-start | bytes 491528 | tf_op jit(solution)/shard_map/ppermute | solution.py:324
  19.8 0.1 pad_add_fusion.meta_ref
  19.8 4.6 %collective-permute-start = (s32[1,33]{1,0:T(1,128)S(1)}, s32[1,33]{1,0:T(1,128)S(1)}, u32[]{:S(2)}, u32[]{:S(2)}) collective-permute-start(s32[1,33]{1,0:T(1,128)S(1)} %pad_add_fusion.meta_ref), channel_id=1, source_target_pairs={{0,32},{32,64},{64,96},{96,128},{128,160},{160,192},{192,224},{224... | collective-permute-start | bytes 404 | tf_op jit(solution)/shard_map/ppermute | solution.py:322
  24.4 0.0 collective-permute-done.1.win_ref
  24.5 0.8 %norm_rows.1 = (f32[128,1]{1,0:T(8,128)S(1)}, f32[128,16]{1,0:T(8,128)S(1)}) custom-call(bf16[128,5120]{1,0:T(8,128)(2,1)S(1)} %bitcast.9, bf16[16,5120]{1,0:T(8,128)(2,1)S(1)} %collective-permute-done.1.win_ref), custom_call_target="tpu_custom_call" | custom-call | flops 20971520 | bytes 1310720 | tf_op jit(solution)/shard_map/norm_rows/pallas_call | solution.py:200
  25.3 2.2 %collective-permute-done.2.wout_ref = bf16[16,5120]{1,0:T(8,128)(2,1)S(1)} collective-permute-done((bf16[16,5120]{1,0:T(8,128)(2,1)S(1)}, bf16[16,5120]{1,0:T(8,128)(2,1)S(1)}, u32[]{:S(2)}, u32[]{:S(2)}) %collective-permute-start.2) | collective-permute-done | bytes 163872 | tf_op jit(solution)/shard_map/ppermute | solution.py:324
  27.5 8.1 %all-to-all-done.blocks_ref = bf16[32,160,128]{2,1,0:T(8,128)(2,1)S(1)} async-done(((bf16[32,160,128]{2,1,0:T(8,128)(2,1)}), bf16[32,160,128]{2,1,0:T(8,128)(2,1)S(1)}, u32[]{:S(2)}, u32[]{:S(2)}) %all-to-all-start) | async-done | bytes 1310752 | tf_op jit(solution)/shard_map/all_to_all | solution.py:310
  35.6 1.3 %collective-permute-start.4 = (bf16[32,160,128]{2,1,0:T(8,128)(2,1)S(1)}, bf16[32,160,128]{2,1,0:T(8,128)(2,1)S(1)}, u32[]{:S(2)}, u32[]{:S(2)}) collective-permute-start(bf16[32,160,128]{2,1,0:T(8,128)(2,1)S(1)} %all-to-all-done.blocks_ref), channel_id=1, source_target_pairs={{32,0},{64,32},{96,64},{128,96},{160,128},{192,160},{224,192},{256... | collective-permute-start | bytes 3932168 | tf_op jit(solution)/shard_map/ppermute | solution.py:330
  36.9 0.0 collective-permute-done.meta_ref
  36.9 3.1 %adapter_backward.1 = bf16[32,8,640]{2,1,0:T(8,128)(2,1)S(1)} custom-call(s32[1,33]{1,0:T(1,128)S(1)} %collective-permute-done.meta_ref, bf16[32,160,128]{2,1,0:T(8,128)(2,1)S(1)} %all-to-all-done.blocks_ref, bf16[128,5120]{1,0:T(8,128)(2,1)} %collective-permute-done.3.rows_ref, bf16[16,5120]{1,0:T(8,128)(2,1)S(1)} %bitcast.12, bf16[16,5120]{1,0:T(8,128)(2,1)S(1)} %bitcast.14), custom_call_target="tpu_custom_call" | custom-call | flops 99999997952 | bytes 200000000 | tf_op jit(solution)/shard_map/adapter_backward/pallas_call | solution.py:167
  40.0 14.2 %all_to_all.15.pieces_ref = bf16[32,8,640]{2,1,0:T(8,128)(2,1)S(1)} all-to-all(bf16[32,8,640]{2,1,0:T(8,128)(2,1)S(1)} %adapter_backward.1), channel_id=1, replica_groups=mesh['section'=16,'peer'=32] {'peer'}, dimensions={0} | all-to-all | bytes 655360 | tf_op jit(solution)/shard_map/all_to_all | solution.py:310
  54.2 0.1 sum_pieces.1
  54.3 13.1 %all_to_all.16.pieces_ref = bf16[32,8,640]{2,1,0:T(8,128)(2,1)S(1)} all-to-all(bf16[32,8,640]{2,1,0:T(8,128)(2,1)S(1)} %sum_pieces.1), channel_id=1, replica_groups=mesh['section'=16,'peer'=32] {'peer'}, dimensions={0} | all-to-all | bytes 655360 | tf_op jit(solution)/shard_map/all_to_all | solution.py:310
  67.4 0.9 %join_pieces.1 = (f32[16,5120]{1,0:T(8,128)}, f32[16,5120]{1,0:T(8,128)}) custom-call(bf16[32,8,640]{2,1,0:T(8,128)(2,1)S(1)} %all_to_all.16.pieces_ref), custom_call_target="tpu_custom_call" | custom-call | flops 163840 | bytes 983040 | tf_op jit(solution)/shard_map/join_pieces/pallas_call | solution.py:298
  68.2 0.0 collective-permute-done.4.blocks_ref
  68.2 2.9 %row_grads.1 = bf16[128,5120]{1,0:T(8,128)(2,1)} custom-call(s32[1,33]{1,0:T(1,128)S(1)} %pad_add_fusion.meta_ref, bf16[32,160,128]{2,1,0:T(8,128)(2,1)S(1)} %collective-permute-done.4.blocks_ref, bf16[128,5120]{1,0:T(8,128)(2,1)S(1)} %bitcast.10, bf16[16,5120]{1,0:T(8,128)(2,1)S(1)} %collective-permute-done.1.win_ref, ...), custom_call_target="tpu_custom_call" | custom-call | flops 20971520 | bytes 2621440 | tf_op jit(solution)/shard_map/row_grads/pallas_call | solution.py:255
  (5 shorter events, 0.0 us)
Async XLA Ops:
  0.6 36.2 %collective-permute-start.3 = (bf16[128,5120]{1,0:T(8,128)(2,1)}, bf16[128,5120]{1,0:T(8,128)(2,1)}, u32[]{:S(2)}, u32[]{:S(2)}) collective-permute-start(bf16[128,5120]{1,0:T(8,128)(2,1)} %bitcast.8), channel_id=1, source_target_pairs={{0,32},{32,64},{64,96},{96,128},{128,160},{160,192},{192,224},{224... | collective-permute-start | bytes 3932168 | tf_op jit(solution)/shard_map/ppermute | solution.py:320
  8.2 8.2 %copy-start.1 = (bf16[1,16,5120]{2,1,0:T(8,128)(2,1)S(1)}, bf16[1,16,5120]{2,1,0:T(8,128)(2,1)}, u32[]{:S(2)}) copy-start(bf16[1,16,5120]{2,1,0:T(8,128)(2,1)} %param.8) | copy-start | bytes 491524
  8.3 9.5 %copy-start.2 = (bf16[1,16,5120]{2,1,0:T(8,128)(2,1)S(1)}, bf16[1,16,5120]{2,1,0:T(8,128)(2,1)}, u32[]{:S(2)}) copy-start(bf16[1,16,5120]{2,1,0:T(8,128)(2,1)} %param.9) | copy-start | bytes 491524
  8.3 11.5 %copy-start.3 = (s32[1,1,32,1]{2,3,1,0:T(1,128)S(1)}, s32[1,1,32,1]{2,3,1,0:T(1,128)}, u32[]{:S(2)}) copy-start(s32[1,1,32,1]{2,3,1,0:T(1,128)} %param.10) | copy-start | bytes 388
  8.3 16.2 %copy-start = (bf16[1,1,128,5120]{3,2,1,0:T(8,128)(2,1)S(1)}, bf16[1,1,128,5120]{3,2,1,0:T(8,128)(2,1)}, u32[]{:S(2)}) copy-start(bf16[1,1,128,5120]{3,2,1,0:T(8,128)(2,1)} %param.6) | copy-start | bytes 3932164
  8.3 27.3 %all-to-all-start = ((bf16[32,160,128]{2,1,0:T(8,128)(2,1)}), bf16[32,160,128]{2,1,0:T(8,128)(2,1)S(1)}, u32[]{:S(2)}, u32[]{:S(2)}) async-start(bf16[32,160,128]{2,1,0:T(8,128)(2,1)} %pack_blocks.1), calls=%async_computation | async-start | bytes 2621440 | tf_op jit(solution)/shard_map/all_to_all | solution.py:310
  16.5 8.0 %collective-permute-start.1 = (bf16[16,5120]{1,0:T(8,128)(2,1)S(1)}, bf16[16,5120]{1,0:T(8,128)(2,1)S(1)}, u32[]{:S(2)}, u32[]{:S(2)}) collective-permute-start(bf16[16,5120]{1,0:T(8,128)(2,1)S(1)} %bitcast.11), channel_id=1, source_target_pairs={{32,0},{64,32},{96,64},{128,96},{160,128},{192,160},{224,192},{256... | collective-permute-start | bytes 491528 | tf_op jit(solution)/shard_map/ppermute | solution.py:323
  17.8 9.7 %collective-permute-start.2 = (bf16[16,5120]{1,0:T(8,128)(2,1)S(1)}, bf16[16,5120]{1,0:T(8,128)(2,1)S(1)}, u32[]{:S(2)}, u32[]{:S(2)}) collective-permute-start(bf16[16,5120]{1,0:T(8,128)(2,1)S(1)} %bitcast.13), channel_id=1, source_target_pairs={{32,0},{64,32},{96,64},{128,96},{160,128},{192,160},{224,192},{256... | collective-permute-start | bytes 491528 | tf_op jit(solution)/shard_map/ppermute | solution.py:324
  19.8 17.0 %collective-permute-start = (s32[1,33]{1,0:T(1,128)S(1)}, s32[1,33]{1,0:T(1,128)S(1)}, u32[]{:S(2)}, u32[]{:S(2)}) collective-permute-start(s32[1,33]{1,0:T(1,128)S(1)} %pad_add_fusion.meta_ref), channel_id=1, source_target_pairs={{0,32},{32,64},{64,96},{96,128},{128,160},{160,192},{192,224},{224... | collective-permute-start | bytes 404 | tf_op jit(solution)/shard_map/ppermute | solution.py:322
  35.6 32.7 %collective-permute-start.4 = (bf16[32,160,128]{2,1,0:T(8,128)(2,1)S(1)}, bf16[32,160,128]{2,1,0:T(8,128)(2,1)S(1)}, u32[]{:S(2)}, u32[]{:S(2)}) collective-permute-start(bf16[32,160,128]{2,1,0:T(8,128)(2,1)S(1)} %all-to-all-done.blocks_ref), channel_id=1, source_target_pairs={{32,0},{64,32},{96,64},{128,96},{160,128},{192,160},{224,192},{256... | collective-permute-start | bytes 3932168 | tf_op jit(solution)/shard_map/ppermute | solution.py:330
